TPU v7x, 32 devices: a whole 2x2x4 slice. The times are simulated.
32 devices in a mesh: seq: 8 (over y, x, core), wt: 4 (over z).
Axes of the slice: x: 2, y: 2, z: 4, core: 2. Of those that a mesh axis runs over, the one named last changes fastest.
Arguments:
- block_input: bfloat16 [10240, 1024], P(('seq', 'wt')), may hold values from -6 to 6
- positions: int32 [10240], P(('seq', 'wt')), may hold values from 0 to 9919, as said below
- norm_gain_attn: bfloat16 [1024], P(('seq', 'wt')), may hold values from 0.5 to 1.5
- w_qkv: bfloat16 [1024, 3072], P(('seq', 'wt')), may hold values from -0.1875 to 0.1875
- w_out: bfloat16 [1024, 1024], P(('seq', 'wt')), may hold values from -0.5 to 0.5
- norm_gain_mlp: bfloat16 [1024], P(('seq', 'wt')), may hold values from 0.5 to 1.5
- w_in: bfloat16 [1024, 5248], P(('seq', 'wt')), may hold values from -0.1875 to 0.1875
- w_down: bfloat16 [1024, 2624], P(('seq', 'wt')), may hold values from -0.125 to 0.125
- cotangent: bfloat16 [10240, 1024], P(('seq', 'wt')), may hold values from -6 to 6
Outputs:
- block_output: bfloat16 [10240, 1024], P(('seq', 'wt'))
- input_grad: bfloat16 [10240, 1024], P(('seq', 'wt'))
- grad_gain_attn: float32 [1024], P(('seq', 'wt'))
- grad_qkv: float32 [1024, 3072], P(('seq', 'wt'))
- grad_out: float32 [1024, 1024], P(('seq', 'wt'))
- grad_gain_mlp: float32 [1024], P(('seq', 'wt'))
- grad_in: float32 [1024, 5248], P(('seq', 'wt'))
- grad_down: float32 [1024, 2624], P(('seq', 'wt'))
Inputs may be any that keep to these rules, and one draw needn't show every extreme that they name: positions count up by one from 0 within each document, and a document begins at token 0; one long document begins inside the first aligned block of 320 tokens at an offset of 64 to 256 and ends at the same offset inside the last aligned block, so that it holds 9920 tokens; the tokens before it and after it form further documents of varying lengths.
All inputs are finite; a program needn't handle non-finite values.
Results may differ from a plain program's by a relative error of at most 0.015.
Values may be sent and summed in bfloat16 or wider, within the bound.
A program may use at most 256 MiB of HBM per device.

v0:
```python
import jax
import jax.numpy as jnp
from jax import lax
from jax.sharding import PartitionSpec as P

HEADS = 16
HEAD_DIM = 64
WING = 64


EPSILON = 1e-05


def padded_2(block, sides, width):
    for axis, dim in sides:
        count = lax.axis_size(axis)
        forward = [(i, i + 1) for i in range(count - 1)]
        backward = [(target, source) for source, target in forward]
        low = lax.ppermute(
            lax.slice_in_dim(block, block.shape[dim] - width, None, axis=dim), axis, forward
        )
        high = lax.ppermute(lax.slice_in_dim(block, 0, width, axis=dim), axis, backward)
        block = jnp.concatenate([low, block, high], axis=dim)
    return block


def shifted(block, axis, distance):
    devices = range(lax.axis_size(axis))
    route = [(i - distance, i) for i in devices if i - distance in devices]
    return lax.ppermute(block, axis, route)


def layer_norm(rows, gain):
    centered = rows - jnp.mean(rows, axis=-1, keepdims=True)
    spread = jnp.mean(centered * centered, axis=-1, keepdims=True)
    return centered * lax.rsqrt(spread + EPSILON) * gain


def rotate_half(vectors):
    middle = vectors.shape[-1] // 2
    return jnp.concatenate([-vectors[..., middle:], vectors[..., :middle]], axis=-1)


def angles(positions, head_width):
    middle = head_width // 2
    freqs = 10000.0 ** (-2.0 * jnp.arange(middle, dtype=jnp.float32) / head_width)
    phase = positions.astype(jnp.float32)[:, None] * freqs[None, :]
    phase = jnp.concatenate([phase, phase], axis=-1)[:, None, :]
    return (jnp.cos(phase), jnp.sin(phase))


def rotary(vectors, cosine, sine):
    return vectors * cosine + rotate_half(vectors) * sine


def rotary_back(grads, cosine, sine):
    return grads * cosine - rotate_half(grads * sine)


def gated(first, second):
    return jax.nn.gelu(first, approximate=False) * second


def gather_weights(gain_attn, w_qkv, w_out, gain_mlp, w_in, w_down):
    return (
        lax.all_gather(gain_attn, ("seq", "wt"), axis=0, tiled=True),
        lax.all_gather(w_qkv, ("seq", "wt"), axis=0, tiled=True),
        lax.all_gather(w_out, ("seq", "wt"), axis=0, tiled=True),
        lax.all_gather(gain_mlp, ("seq", "wt"), axis=0, tiled=True),
        lax.all_gather(w_in, ("seq", "wt"), axis=0, tiled=True),
        lax.all_gather(w_down, ("seq", "wt"), axis=0, tiled=True),
    )


def scatter_grads(gain_attn, w_qkv, w_out, gain_mlp, w_in, w_down):
    return (
        lax.psum_scatter(gain_attn, ("seq", "wt"), scatter_dimension=0, tiled=True),
        lax.psum_scatter(w_qkv, ("seq", "wt"), scatter_dimension=0, tiled=True),
        lax.psum_scatter(w_out, ("seq", "wt"), scatter_dimension=0, tiled=True),
        lax.psum_scatter(gain_mlp, ("seq", "wt"), scatter_dimension=0, tiled=True),
        lax.psum_scatter(w_in, ("seq", "wt"), scatter_dimension=0, tiled=True),
        lax.psum_scatter(w_down, ("seq", "wt"), scatter_dimension=0, tiled=True),
    )


def block_mask(positions, block_start, block_rows, token_total, at_first, at_last):
    key_count = block_rows + 2 * WING
    query_index = block_start + jnp.arange(block_rows, dtype=jnp.int32)
    key_index = block_start - WING + jnp.arange(key_count, dtype=jnp.int32)
    padded = jnp.pad(positions, (WING, WING))
    offset = query_index[:, None] - key_index[None, :]
    inside = (key_index >= 0) & (key_index < token_total)
    same_doc = jnp.where(inside[None, :], positions[:, None] - padded[None, :] == offset, True)
    present = ((key_index >= 0) | jnp.logical_not(at_first)) & (
        (key_index < token_total) | jnp.logical_not(at_last)
    )
    return (jnp.abs(offset) <= WING) & same_doc & present[None, :]


def block_probs(query_block, key_block, allowed):
    scaling = HEAD_DIM ** (-0.5)
    scores = (
        jnp.einsum("qhd,khd->hqk", query_block, key_block, preferred_element_type=jnp.float32)
        * scaling
    )
    scores = jnp.where(allowed[None], scores, -1e30)
    largest = jnp.max(scores, axis=-1, keepdims=True)
    weights = jnp.exp(scores - largest)
    return weights / jnp.sum(weights, axis=-1, keepdims=True)


def on_device(
    block_input, positions, norm_gain_attn, w_qkv, w_out, norm_gain_mlp, w_in, w_down, cotangent
):
    token_total = block_input.shape[0]
    width = block_input.shape[1]
    scaling = HEAD_DIM ** (-0.5)
    gain_attn, full_qkv, full_out, gain_mlp, full_in, full_down = gather_weights(
        norm_gain_attn, w_qkv, w_out, norm_gain_mlp, w_in, w_down
    )
    hidden_units = full_down.shape[1]
    device_index = lax.axis_index(("seq", "wt"))
    at_first = device_index == 0
    at_last = device_index == lax.axis_size(("seq", "wt")) - 1
    inputs = block_input.astype(jnp.float32)
    normed_one, norm_one_back = jax.vjp(layer_norm, inputs, gain_attn.astype(jnp.float32))
    act_one = normed_one.astype(jnp.bfloat16)
    qkv = jnp.dot(act_one, full_qkv, preferred_element_type=jnp.float32)
    cosine, sine = angles(positions, HEAD_DIM)
    query_rot = rotary(qkv[:, :width].reshape(token_total, HEADS, HEAD_DIM), cosine, sine).astype(
        jnp.bfloat16
    )
    key_rot = rotary(
        qkv[:, width : 2 * width].reshape(token_total, HEADS, HEAD_DIM), cosine, sine
    ).astype(jnp.bfloat16)
    value_low = qkv[:, 2 * width :].astype(jnp.bfloat16)
    paired = jnp.concatenate([key_rot.reshape(token_total, width), value_low], axis=1)
    edged = padded_2(paired, ((("seq", "wt"), 0),), WING)
    key_ext = edged[:, :width].reshape(-1, HEADS, HEAD_DIM)
    value_ext = edged[:, width:].reshape(-1, HEADS, HEAD_DIM)
    block_rows = min(512, token_total)
    starts = jnp.arange(token_total // block_rows, dtype=jnp.int32) * block_rows

    def slices(block_start):
        allowed = block_mask(positions, block_start, block_rows, token_total, at_first, at_last)
        return (query_rot, key_ext, value_ext, allowed)

    def forward_block(block_start):
        query_block, key_block, value_block, allowed = slices(block_start)
        probs = block_probs(query_block, key_block, allowed)
        mixed = jnp.einsum(
            "hqk,khd->qhd",
            probs.astype(jnp.bfloat16),
            value_block,
            preferred_element_type=jnp.float32,
        )
        return (mixed, probs)

    mixed, stored = lax.map(forward_block, starts)
    attn = mixed.reshape(token_total, width).astype(jnp.bfloat16)
    resid = inputs + jnp.dot(attn, full_out, preferred_element_type=jnp.float32)
    normed_two, norm_two_back = jax.vjp(layer_norm, resid, gain_mlp.astype(jnp.float32))
    act_two = normed_two.astype(jnp.bfloat16)
    upward = jnp.dot(act_two, full_in, preferred_element_type=jnp.float32)
    gated_value, gated_back = jax.vjp(gated, upward[:, :hidden_units], upward[:, hidden_units:])
    hidden = gated_value.astype(jnp.bfloat16)
    output = resid + jnp.einsum("tf,df->td", hidden, full_down, preferred_element_type=jnp.float32)
    block_output = output.astype(jnp.bfloat16)
    grad_down = jnp.einsum("td,tf->df", cotangent, hidden, preferred_element_type=jnp.float32)
    dhidden = jnp.dot(cotangent, full_down, preferred_element_type=jnp.float32)
    dfirst, dsecond = gated_back(dhidden)
    dupward = jnp.concatenate([dfirst, dsecond], axis=1).astype(jnp.bfloat16)
    grad_in = jnp.einsum("td,tf->df", act_two, dupward, preferred_element_type=jnp.float32)
    dact_two = jnp.einsum("tf,df->td", dupward, full_in, preferred_element_type=jnp.float32)
    dresid_norm, grad_gain_mlp = norm_two_back(dact_two)
    dresid = cotangent.astype(jnp.float32) + dresid_norm
    dresid_low = dresid.astype(jnp.bfloat16)
    grad_out = jnp.einsum("ti,to->io", attn, dresid_low, preferred_element_type=jnp.float32)
    dattn = jnp.einsum("to,io->ti", dresid_low, full_out, preferred_element_type=jnp.float32)
    dattn = dattn.astype(jnp.bfloat16).reshape(token_total, HEADS, HEAD_DIM)
    zeros_ext = jnp.zeros((token_total + 2 * WING, HEADS, HEAD_DIM), jnp.float32)

    def backward_block(carry, block_start):
        key_grad, value_grad = carry
        query_block, key_block, value_block, allowed = slices(block_start)
        probs = lax.dynamic_index_in_dim(stored, block_start // block_rows, 0, keepdims=False)
        dprobs = jnp.einsum("qhd,khd->hqk", dattn, value_block, preferred_element_type=jnp.float32)
        inner = jnp.sum(probs * dprobs, axis=-1, keepdims=True)
        dscores = (probs * (dprobs - inner)).astype(jnp.bfloat16)
        dquery = (
            jnp.einsum("hqk,khd->qhd", dscores, key_block, preferred_element_type=jnp.float32)
            * scaling
        )
        dkey = (
            jnp.einsum("hqk,qhd->khd", dscores, query_block, preferred_element_type=jnp.float32)
            * scaling
        )
        dvalue = jnp.einsum(
            "hqk,qhd->khd", probs.astype(jnp.bfloat16), dattn, preferred_element_type=jnp.float32
        )
        key_grad = key_grad + dkey
        value_grad = value_grad + dvalue
        return ((key_grad, value_grad), dquery)

    (key_grad, value_grad), dquery = lax.scan(backward_block, (zeros_ext, zeros_ext), starts)
    edge_grad = jnp.concatenate(
        [key_grad.reshape(-1, width), value_grad.reshape(-1, width)], axis=1
    )
    from_next = shifted(edge_grad[:WING].astype(jnp.bfloat16), ("seq", "wt"), -1).astype(
        jnp.float32
    )
    from_prev = shifted(
        edge_grad[token_total + WING :].astype(jnp.bfloat16), ("seq", "wt"), 1
    ).astype(jnp.float32)
    local_grad = edge_grad[WING : WING + token_total]
    local_grad = local_grad.at[:WING].add(from_prev).at[token_total - WING :].add(from_next)
    dquery_all = dquery.reshape(token_total, HEADS, HEAD_DIM)
    dkey_rot = local_grad[:, :width].reshape(token_total, HEADS, HEAD_DIM)
    dqkv = jnp.concatenate(
        [
            rotary_back(dquery_all, cosine, sine).reshape(token_total, width),
            rotary_back(dkey_rot, cosine, sine).reshape(token_total, width),
            local_grad[:, width:],
        ],
        axis=1,
    ).astype(jnp.bfloat16)
    grad_qkv = jnp.einsum("td,tf->df", act_one, dqkv, preferred_element_type=jnp.float32)
    dact_one = jnp.einsum("tf,df->td", dqkv, full_qkv, preferred_element_type=jnp.float32)
    dinput_norm, grad_gain_attn = norm_one_back(dact_one)
    input_grad = (dresid + dinput_norm).astype(jnp.bfloat16)
    shares = scatter_grads(grad_gain_attn, grad_qkv, grad_out, grad_gain_mlp, grad_in, grad_down)
    return (
        block_output,
        input_grad,
        shares[0],
        shares[1],
        shares[2],
        shares[3],
        shares[4],
        shares[5],
    )


def solution(mesh):
    in_specs = (
        P(("seq", "wt"), None),
        P(("seq", "wt")),
        P(("seq", "wt")),
        P(("seq", "wt"), None),
        P(("seq", "wt"), None),
        P(("seq", "wt")),
        P(("seq", "wt"), None),
        P(("seq", "wt"), None),
        P(("seq", "wt"), None),
    )
    out_specs = (
        P(("seq", "wt"), None),
        P(("seq", "wt"), None),
        P(("seq", "wt")),
        P(("seq", "wt"), None),
        P(("seq", "wt"), None),
        P(("seq", "wt")),
        P(("seq", "wt"), None),
        P(("seq", "wt"), None),
    )
    return jax.shard_map(
        on_device, mesh=mesh, in_specs=in_specs, out_specs=out_specs, check_vma=False
    )
```

profile of v0, /device:TPU:0, one launch (start us, length us, event | category | flops | bytes accessed | tf_op | source)
XLA Modules:
  0.0 1268.0 jit_solution(6436189915376502788)
XLA Ops:
  11.7 42.5 %all-reduce.6 = (bf16[1024]{0:T(1024)(128)(2,1)S(1)}, bf16[1024]{0:T(1024)(128)(2,1)S(1)}) all-reduce(bf16[1024]{0:T(1024)(128)(2,1)S(1)} %dynamic-update-slice.6, bf16[1024]{0:T(1024)(128)(2,1)S(1)} %dynamic-update-slice.7), channel_id=1, replica_groups=mesh['seq'=8,'wt'=4] {'seq','wt'}, use_global_device_ids=true, to_apply=%add.1 | all-reduce | flops 2048 | bytes 8192
  59.9 23.5 %all-gather.5.cloned.1.call-done = bf16[1024,3072]{1,0:T(8,128)(2,1)} async-done(((bf16[32,3072]{1,0:T(8,128)(2,1)}), bf16[1024,3072]{1,0:T(8,128)(2,1)}) %all-gather.5.cloned.1.call-update) | async-done | bytes 6291472 | tf_op jit(solution)/shard_map/all_gather | solution.py:67
  117.6 7.6 fusion.72
  125.1 6.3 fusion.30
  131.4 11.5 all-gather.7.cloned.1.call-done
  145.8 86.8 %all-gather.9.cloned.1.call-done = bf16[1024,5248]{1,0:T(8,128)(2,1)} async-done(((bf16[32,5248]{1,0:T(8,128)(2,1)}), bf16[1024,5248]{1,0:T(8,128)(2,1)}) %all-gather.9.cloned.1.call-update) | async-done | bytes 10747920 | tf_op jit(solution)/shard_map/all_gather | solution.py:70
  232.6 9.9 fusion.66
  242.5 57.4 %all-gather.11.cloned.1.call-done = bf16[1024,2624]{1,0:T(8,128)(2,1)} async-done(((bf16[32,2624]{1,0:T(8,128)(2,1)}), bf16[1024,2624]{1,0:T(8,128)(2,1)}) %all-gather.11.cloned.1.call-update) | async-done | bytes 5373968 | tf_op jit(solution)/shard_map/all_gather | solution.py:71
  299.9 13.0 %add_convert_fusion = (bf16[320,2624]{1,0:T(8,128)(2,1)}, f32[320,2624]{1,0:T(8,128)S(1)}, f32[320,2624]{1,0:T(8,128)S(1)}) fusion(f32[320,5248]{1,0:T(8,128)} %fusion.66, bf16[320,1024]{1,0:T(8,128)(2,1)S(1)} %copy-done.4, bf16[1024,2624]{1,0:T(8,128)(2,1)} %all-gather.11.cloned.1.call-done), kind=kOutput, calls=%fused_computation.20 | convolution fusion | flops 1780961280 | bytes 21143552 | tf_op jit(solution)/shard_map/dot_general | solution.py:170
  315.4 8.0 multiply_reduce_fusion.1
  328.9 8.7 convolution_bitcast_fusion
  337.6 12.0 copy.52
  355.5 11.1 multiply_reduce_fusion
  387.2 12.9 %collective-permute-done.2 = bf16[64,2048]{0,1:T(8,128)(2,1)S(1)} collective-permute-done((bf16[64,2048]{0,1:T(8,128)(2,1)S(1)}, bf16[64,2048]{0,1:T(8,128)(2,1)S(1)}, u32[]{:S(2)}, u32[]{:S(2)}) %collective-permute-start.2) | collective-permute-done | bytes 262176 | tf_op jit(solution)/shard_map/ppermute | solution.py:30
  401.4 6.3 scatter-add.6
  407.6 15.2 %collective-permute-done.3 = bf16[64,2048]{0,1:T(8,128)(2,1)} collective-permute-done((bf16[64,2048]{0,1:T(8,128)(2,1)}, bf16[64,2048]{0,1:T(8,128)(2,1)}, u32[]{:S(2)}, u32[]{:S(2)}) %collective-permute-start.3) | collective-permute-done | bytes 262176 | tf_op jit(solution)/shard_map/ppermute | solution.py:30
  431.9 9.2 fusion.43
  441.2 12.8 %fusion.18 = f32[1024,5248]{1,0:T(8,128)} fusion(bf16[320,2624]{1,0:T(8,128)(2,1)} %copy-done.3, bf16[320,2624]{1,0:T(8,128)(2,1)} %get-tuple-element.120, f32[320,1024]{1,0:T(8,128)S(1)} %get-tuple-element.147, f32[1024]{0:T(1024)S(1)} %convert_element_type.83, f32[320]{0:T(512)S(1)} %fusion.54, f32[320]{0:T(512)S(1)} %broadcast_multiply_fusion.4), kind=kOutput, calls=%fused_computation.44 | convolution fusion | flops 3447357440 | bytes 26171904 | tf_op jit(solution)/shard_map/td,tf->df/dot_general | solution.py:173
  454.1 6.2 fusion.33
  460.3 5.8 fusion.37
  467.8 40.7 %all-reduce.5 = (f32[1024]{0:T(1024)S(1)}, f32[1024]{0:T(1024)S(1)}) all-reduce(f32[1024]{0:T(1024)S(1)} %get-tuple-element.112, f32[1024]{0:T(1024)S(1)} %get-tuple-element.110), channel_id=2, replica_groups=mesh['seq'=8,'wt'=4] {'seq','wt'}, use_global_device_ids=true, to_apply=%region_12.13.clone | all-reduce | flops 2048 | bytes 16384
  512.5 123.6 %reduce-scatter.13.cloned.1.call-done = f32[32,2624]{1,0:T(8,128)} async-done(((f32[1024,2624]{1,0:T(8,128)}), f32[32,2624]{1,0:T(8,128)}) %reduce-scatter.13.cloned.1.call-update) | async-done | bytes 335888
  636.1 161.0 %reduce-scatter.7.cloned.1.call-done = f32[32,3072]{1,0:T(8,128)} async-done(((f32[1024,3072]{1,0:T(8,128)}), f32[32,3072]{1,0:T(8,128)}) %reduce-scatter.7.cloned.1.call-update) | async-done | bytes 393232 | tf_op jit(solution)/shard_map/reduce_scatter | solution.py:78
  797.1 463.6 %reduce-scatter.11.cloned.1.call-done = f32[32,5248]{1,0:T(8,128)} async-done(((f32[1024,5248]{1,0:T(8,128)}), f32[32,5248]{1,0:T(8,128)}) %reduce-scatter.11.cloned.1.call-update) | async-done | bytes 671760 | tf_op jit(solution)/shard_map/reduce_scatter | solution.py:81
  (169 shorter events, 97.4 us)
Async XLA Ops:
  7.2 51.1 %copy-start.33 = (s32[320]{0:T(512)S(1)}, s32[320]{0:T(512)}, u32[]{:S(2)}) copy-start(s32[320]{0:T(512)} %param.14) | copy-start | bytes 3844
  7.2 51.1 %copy-start = (bf16[320,1024]{1,0:T(8,128)(2,1)S(1)}, bf16[320,1024]{1,0:T(8,128)(2,1)}, u32[]{:S(2)}) copy-start(bf16[320,1024]{1,0:T(8,128)(2,1)} %param.13) | copy-start | bytes 1966084
  7.2 76.1 %all-gather.5.cloned.1.call-start = ((), (), s32[]{:S(2)}) async-start(), calls=%async_computation.4 | async-start | bytes 6488064 | tf_op jit(solution)/shard_map/all_gather | solution.py:67
  7.9 135.0 %all-gather.7.cloned.1.call-start = ((), (), s32[]{:S(2)}) async-start(), calls=%async_computation.5 | async-start | bytes 2162688 | tf_op jit(solution)/shard_map/all_gather | solution.py:68
  8.7 223.9 %all-gather.9.cloned.1.call-start = ((), (), s32[]{:S(2)}) async-start(), calls=%async_computation.6 | async-start | bytes 11083776 | tf_op jit(solution)/shard_map/all_gather | solution.py:70
  9.4 290.5 %all-gather.11.cloned.1.call-start = ((), (), s32[]{:S(2)}) async-start(), calls=%async_computation.7 | async-start | bytes 5677056 | tf_op jit(solution)/shard_map/all_gather | solution.py:71
  10.0 502.5 %reduce-scatter.9.cloned.1.call-start = ((), (), s32[]{:S(2)}) async-start(), calls=%async_computation.9 | async-start | bytes 4325376 | tf_op jit(solution)/shard_map/reduce_scatter | solution.py:79
  55.9 37.6 %copy-start.22 = (f32[320,64]{0,1:T(8,128)}, f32[320,64]{0,1:T(8,128)S(1)}, u32[]{:S(2)}) copy-start(f32[320,64]{0,1:T(8,128)S(1)} %get-tuple-element.142) | copy-start | bytes 245764
  58.9 29.6 %copy-start.31 = (f32[320]{0:T(512)}, f32[320]{0:T(512)S(1)}, u32[]{:S(2)}) copy-start(f32[320]{0:T(512)S(1)} %fusion.36) | copy-start | bytes 3844
  100.0 10.7 collective-permute-start.1
  101.3 12.6 collective-permute-start
  131.4 14.4 %copy-start.9 = (bf16[16,64,320]{2,1,0:T(8,128)(2,1)}, bf16[16,64,320]{2,1,0:T(8,128)(2,1)S(1)}, u32[]{:S(2)}) copy-start(bf16[16,64,320]{2,1,0:T(8,128)(2,1)S(1)} %fusion.30) | copy-start | bytes 1966084
  145.8 154.1 %copy-start.4 = (bf16[320,1024]{1,0:T(8,128)(2,1)S(1)}, bf16[320,1024]{1,0:T(8,128)(2,1)}, u32[]{:S(2)}) copy-start(bf16[320,1024]{1,0:T(8,128)(2,1)} %param.21) | copy-start | bytes 1966084
  299.9 13.0 %copy-start.2 = (f32[320,5248]{1,0:T(8,128)S(1)}, f32[320,5248]{1,0:T(8,128)}, u32[]{:S(2)}) copy-start(f32[320,5248]{1,0:T(8,128)} %fusion.66) | copy-start | bytes 20152324
  328.9 307.2 %reduce-scatter.13.cloned.1.call-start = ((), (), s32[]{:S(2)}) async-start(), calls=%async_computation.11 | async-start | bytes 11354112
  349.6 447.5 %reduce-scatter.7.cloned.1.call-start = ((), (), s32[]{:S(2)}) async-start(), calls=%async_computation.8 | async-start | bytes 12976128 | tf_op jit(solution)/shard_map/reduce_scatter | solution.py:78
  355.5 11.1 slice-start
  355.5 11.1 slice-start.1
  355.5 11.2 slice-start.2
  376.6 23.5 %collective-permute-start.2 = (bf16[64,2048]{0,1:T(8,128)(2,1)S(1)}, bf16[64,2048]{0,1:T(8,128)(2,1)S(1)}, u32[]{:S(2)}, u32[]{:S(2)}) collective-permute-start(bf16[64,2048]{0,1:T(8,128)(2,1)S(1)} %get-tuple-element.127), channel_id=1, source_target_pairs={{0,1},{1,2},{2,3},{3,4},{4,5},{5,6},{6,7},{7,8},{8,9},{9,10},{10,1... | collective-permute-start | bytes 786440 | tf_op jit(solution)/shard_map/ppermute | solution.py:30
  380.5 42.3 %collective-permute-start.3 = (bf16[64,2048]{0,1:T(8,128)(2,1)}, bf16[64,2048]{0,1:T(8,128)(2,1)}, u32[]{:S(2)}, u32[]{:S(2)}) collective-permute-start(bf16[64,2048]{0,1:T(8,128)(2,1)} %get-tuple-element.126), channel_id=1, source_target_pairs={{1,0},{2,1},{3,2},{4,3},{5,4},{6,5},{7,6},{8,7},{9,8},{10,9},{11,1... | collective-permute-start | bytes 786440 | tf_op jit(solution)/shard_map/ppermute | solution.py:30
  407.6 21.1 %copy-start.24 = (f32[320,64]{0,1:T(8,128)S(1)}, f32[320,64]{0,1:T(8,128)}, u32[]{:S(2)}) copy-start(f32[320,64]{0,1:T(8,128)} %copy-done.22) | copy-start | bytes 245764
  441.1 819.6 %reduce-scatter.11.cloned.1.call-start = ((), (), s32[]{:S(2)}) async-start(), calls=%async_computation.10 | async-start | bytes 22167552 | tf_op jit(solution)/shard_map/reduce_scatter | solution.py:81
  460.2 49.5 %copy-start.6 = (bf16[320,1024]{1,0:T(8,128)(2,1)S(1)}, bf16[320,1024]{1,0:T(8,128)(2,1)}, u32[]{:S(2)}) copy-start(bf16[320,1024]{1,0:T(8,128)(2,1)} %param.21) | copy-start | bytes 1966084
  (25 other events, 85.9 us)
Sparse Core Ops, SparseCore 0:
  10.9 72.3 all-gather.4
  86.2 56.6 all-gather.6
  145.8 86.7 all-gather.8
  235.2 64.6 all-gather.10
  329.0 157.5 reduce-scatter.8
  493.0 143.0 reduce-scatter.12
  642.7 154.3 reduce-scatter.6
  800.1 460.5 reduce-scatter.10
where the time goes:
time: 1270 us
  waiting for transfers between devices  962 us (76%)
  matrix products  118 us (9%)
  blocking collectives  83.2 us (7%)
  local copies, waits for them, and re-layouts  46.5 us (4%)
  other arithmetic  32 us (3%)
  between operations  15.2 us (1%)
    reduce_scatter x1, waiting for transfers between devices, scatter_grads(): lax.psum_scatter(w_in, ('seq', 'wt'), scatter_dimension=0, tiled=True)  464 us
    reduce_scatter x1, waiting for transfers between devices, scatter_grads(): lax.psum_scatter(w_qkv, ('seq', 'wt'), scatter_dimension=0, tiled=True)  161 us
    unnamed x9, waiting for transfers between devices  126 us
    all_gather x1, waiting for transfers between devices, gather_weights(): lax.all_gather(w_in, ('seq', 'wt'), axis=0, tiled=True)  86.8 us
    unnamed x2, blocking collectives  83.2 us
    all_gather x1, waiting for transfers between devices, gather_weights(): lax.all_gather(w_down, ('seq', 'wt'), axis=0, tiled=True)  57.4 us
    ppermute x2, waiting for transfers between devices, shifted(): return lax.ppermute(block, axis, route)  28.1 us
  transfers between devices with their start and end apart: 12, of which 11 were waited for; matrix products, arithmetic and copies ran while one was open for 13% of the time, Pallas kernels for 0%

commit v1 on v0

--- a/solution.py
+++ b/solution.py
@@ -61,26 +61,84 @@
     return jax.nn.gelu(first, approximate=False) * second
 
 
-def gather_weights(gain_attn, w_qkv, w_out, gain_mlp, w_in, w_down):
-    return (
-        lax.all_gather(gain_attn, ("seq", "wt"), axis=0, tiled=True),
-        lax.all_gather(w_qkv, ("seq", "wt"), axis=0, tiled=True),
-        lax.all_gather(w_out, ("seq", "wt"), axis=0, tiled=True),
-        lax.all_gather(gain_mlp, ("seq", "wt"), axis=0, tiled=True),
-        lax.all_gather(w_in, ("seq", "wt"), axis=0, tiled=True),
-        lax.all_gather(w_down, ("seq", "wt"), axis=0, tiled=True),
-    )
-
-
-def scatter_grads(gain_attn, w_qkv, w_out, gain_mlp, w_in, w_down):
-    return (
-        lax.psum_scatter(gain_attn, ("seq", "wt"), scatter_dimension=0, tiled=True),
-        lax.psum_scatter(w_qkv, ("seq", "wt"), scatter_dimension=0, tiled=True),
-        lax.psum_scatter(w_out, ("seq", "wt"), scatter_dimension=0, tiled=True),
-        lax.psum_scatter(gain_mlp, ("seq", "wt"), scatter_dimension=0, tiled=True),
-        lax.psum_scatter(w_in, ("seq", "wt"), scatter_dimension=0, tiled=True),
-        lax.psum_scatter(w_down, ("seq", "wt"), scatter_dimension=0, tiled=True),
-    )
+def device_count():
+    return lax.axis_size(("seq", "wt"))
+
+
+def swapped(block, mask):
+    route = [(i, i ^ mask) for i in range(device_count())]
+    return lax.ppermute(block, ("seq", "wt"), route)
+
+
+def stage_bits(flip):
+    near = lax.axis_size("wt")
+    far = []
+    bit = near
+    while bit < device_count():
+        far.append(bit)
+        bit *= 2
+    first, rest = far[0], far[1:]
+    return near, first, rest[::-1] if flip else rest
+
+
+def gather_rel(block, flip):
+    near, first, rest = stage_bits(flip)
+    levels = len(rest) + 1
+    held = jnp.concatenate([block] + [swapped(block, j) for j in range(1, near)], axis=0)
+    held = held.reshape((1,) * levels + held.shape)
+    for bit in rest + [first]:
+        axis = levels - 1 - ((bit // near).bit_length() - 1)
+        held = jnp.concatenate([held, swapped(held, bit)], axis=axis)
+    return held.reshape(-1, block.shape[1])
+
+
+def scatter_rel(left, right, flip):
+    near, first, rest = stage_bits(flip)
+    rows = left.shape[1] // device_count()
+    levels = len(rest) + 1
+    tokens = left.shape[0]
+    parts = left.reshape((tokens,) + (2,) * levels + (near * rows,))
+    first_axis = levels
+    second_axis = levels - ((rest[0] // near).bit_length() - 1)
+
+    def part(core, second):
+        piece = lax.slice_in_dim(parts, core, core + 1, axis=first_axis)
+        piece = lax.slice_in_dim(piece, second, second + 1, axis=second_axis)
+        return piece.reshape(tokens, -1)
+
+    def product(core, second):
+        return lax.dot_general(
+            part(core, second),
+            right,
+            (((0,), (0,)), ((), ())),
+            preferred_element_type=jnp.float32,
+        )
+
+    got_far = swapped(product(1, 1).astype(jnp.bfloat16), first)
+    got_near = swapped(product(1, 0).astype(jnp.bfloat16), first)
+    far = (product(0, 1) + got_far.astype(jnp.float32)).astype(jnp.bfloat16)
+    got = swapped(far, rest[0])
+    total = product(0, 0) + got_near.astype(jnp.float32) + got.astype(jnp.float32)
+    remaining = sorted(rest[1:], reverse=True)
+    total = total.reshape((2,) * len(remaining) + (near, rows, right.shape[1]))
+    for bit in rest[1:]:
+        axis = remaining.index(bit)
+        keep = lax.slice_in_dim(total, 0, 1, axis=axis)
+        send = lax.slice_in_dim(total, 1, 2, axis=axis).astype(jnp.bfloat16)
+        total = keep + swapped(send, bit).astype(jnp.float32)
+    total = total.reshape(near, rows, right.shape[1])
+    result = total[0]
+    for j in range(1, near):
+        result = result + swapped(total[j].astype(jnp.bfloat16), j).astype(jnp.float32)
+    return result
+
+
+def scatter_gains(gains):
+    total = gains.reshape(gains.shape[0], device_count(), -1).swapaxes(0, 1)
+    while total.shape[0] > 1:
+        half = total.shape[0] // 2
+        total = total[:half] + swapped(total[half:], half)
+    return total[0]
 
 
 def block_mask(positions, block_start, block_rows, token_total, at_first, at_last):
@@ -115,17 +173,41 @@
     token_total = block_input.shape[0]
     width = block_input.shape[1]
     scaling = HEAD_DIM ** (-0.5)
-    gain_attn, full_qkv, full_out, gain_mlp, full_in, full_down = gather_weights(
-        norm_gain_attn, w_qkv, w_out, norm_gain_mlp, w_in, w_down
-    )
-    hidden_units = full_down.shape[1]
     device_index = lax.axis_index(("seq", "wt"))
+    hidden_units = w_down.shape[1]
+    cut = w_qkv.shape[1] // 2
+    gains = jnp.stack([norm_gain_attn, norm_gain_mlp], axis=1)
+    gains = jnp.pad(gains, ((0, 0), (0, 126)))
+    full_one = gather_rel(jnp.concatenate([w_qkv[:, :cut], gains], axis=1), False)
+    full_two = gather_rel(w_qkv[:, cut:], True)
+    full_out = gather_rel(w_out, False)
+    full_first = gather_rel(w_in[:, :hidden_units], False)
+    full_second = gather_rel(w_in[:, hidden_units:], True)
+    full_down = gather_rel(w_down, True)
+    gain_attn = full_one[:, cut]
+    gain_mlp = full_one[:, cut + 1]
+    full_one = full_one[:, :cut]
+    order = jnp.arange(width, dtype=jnp.int32) ^ (device_index * w_out.shape[0])
+    swap = (order[:, None] == jnp.arange(width, dtype=jnp.int32)[None, :]).astype(jnp.bfloat16)
+
+    def reorder(rows):
+        return jnp.dot(rows, swap, preferred_element_type=jnp.float32).astype(jnp.bfloat16)
+
+    full_out = reorder(full_out)
+    block_input = reorder(block_input)
+    cotangent = reorder(cotangent)
     at_first = device_index == 0
     at_last = device_index == lax.axis_size(("seq", "wt")) - 1
     inputs = block_input.astype(jnp.float32)
     normed_one, norm_one_back = jax.vjp(layer_norm, inputs, gain_attn.astype(jnp.float32))
     act_one = normed_one.astype(jnp.bfloat16)
-    qkv = jnp.dot(act_one, full_qkv, preferred_element_type=jnp.float32)
+    qkv = jnp.concatenate(
+        [
+            jnp.dot(act_one, full_one, preferred_element_type=jnp.float32),
+            jnp.dot(act_one, full_two, preferred_element_type=jnp.float32),
+        ],
+        axis=1,
+    )
     cosine, sine = angles(positions, HEAD_DIM)
     query_rot = rotary(qkv[:, :width].reshape(token_total, HEADS, HEAD_DIM), cosine, sine).astype(
         jnp.bfloat16
@@ -157,27 +239,33 @@
         return (mixed, probs)
 
     mixed, stored = lax.map(forward_block, starts)
-    attn = mixed.reshape(token_total, width).astype(jnp.bfloat16)
+    attn = reorder(mixed.reshape(token_total, width).astype(jnp.bfloat16))
     resid = inputs + jnp.dot(attn, full_out, preferred_element_type=jnp.float32)
     normed_two, norm_two_back = jax.vjp(layer_norm, resid, gain_mlp.astype(jnp.float32))
     act_two = normed_two.astype(jnp.bfloat16)
-    upward = jnp.dot(act_two, full_in, preferred_element_type=jnp.float32)
-    gated_value, gated_back = jax.vjp(gated, upward[:, :hidden_units], upward[:, hidden_units:])
+    first = jnp.dot(act_two, full_first, preferred_element_type=jnp.float32)
+    second = jnp.dot(act_two, full_second, preferred_element_type=jnp.float32)
+    gated_value, gated_back = jax.vjp(gated, first, second)
     hidden = gated_value.astype(jnp.bfloat16)
     output = resid + jnp.einsum("tf,df->td", hidden, full_down, preferred_element_type=jnp.float32)
-    block_output = output.astype(jnp.bfloat16)
-    grad_down = jnp.einsum("td,tf->df", cotangent, hidden, preferred_element_type=jnp.float32)
+    block_output = reorder(output.astype(jnp.bfloat16))
+    grad_down = scatter_rel(cotangent, hidden, True)
     dhidden = jnp.dot(cotangent, full_down, preferred_element_type=jnp.float32)
     dfirst, dsecond = gated_back(dhidden)
-    dupward = jnp.concatenate([dfirst, dsecond], axis=1).astype(jnp.bfloat16)
-    grad_in = jnp.einsum("td,tf->df", act_two, dupward, preferred_element_type=jnp.float32)
-    dact_two = jnp.einsum("tf,df->td", dupward, full_in, preferred_element_type=jnp.float32)
+    dfirst = dfirst.astype(jnp.bfloat16)
+    dsecond = dsecond.astype(jnp.bfloat16)
+    grad_in = jnp.concatenate(
+        [scatter_rel(act_two, dfirst, False), scatter_rel(act_two, dsecond, True)], axis=1
+    )
+    dact_two = jnp.einsum(
+        "tf,df->td", dfirst, full_first, preferred_element_type=jnp.float32
+    ) + jnp.einsum("tf,df->td", dsecond, full_second, preferred_element_type=jnp.float32)
     dresid_norm, grad_gain_mlp = norm_two_back(dact_two)
     dresid = cotangent.astype(jnp.float32) + dresid_norm
     dresid_low = dresid.astype(jnp.bfloat16)
-    grad_out = jnp.einsum("ti,to->io", attn, dresid_low, preferred_element_type=jnp.float32)
+    grad_out = scatter_rel(attn, reorder(dresid_low), False)
     dattn = jnp.einsum("to,io->ti", dresid_low, full_out, preferred_element_type=jnp.float32)
-    dattn = dattn.astype(jnp.bfloat16).reshape(token_total, HEADS, HEAD_DIM)
+    dattn = reorder(dattn.astype(jnp.bfloat16)).reshape(token_total, HEADS, HEAD_DIM)
     zeros_ext = jnp.zeros((token_total + 2 * WING, HEADS, HEAD_DIM), jnp.float32)
 
     def backward_block(carry, block_start):
@@ -224,20 +312,28 @@
         ],
         axis=1,
     ).astype(jnp.bfloat16)
-    grad_qkv = jnp.einsum("td,tf->df", act_one, dqkv, preferred_element_type=jnp.float32)
-    dact_one = jnp.einsum("tf,df->td", dqkv, full_qkv, preferred_element_type=jnp.float32)
+    grad_qkv = jnp.concatenate(
+        [
+            scatter_rel(act_one, dqkv[:, :cut], False),
+            scatter_rel(act_one, dqkv[:, cut:], True),
+        ],
+        axis=1,
+    )
+    dact_one = jnp.einsum(
+        "tf,df->td", dqkv[:, :cut], full_one, preferred_element_type=jnp.float32
+    ) + jnp.einsum("tf,df->td", dqkv[:, cut:], full_two, preferred_element_type=jnp.float32)
     dinput_norm, grad_gain_attn = norm_one_back(dact_one)
-    input_grad = (dresid + dinput_norm).astype(jnp.bfloat16)
-    shares = scatter_grads(grad_gain_attn, grad_qkv, grad_out, grad_gain_mlp, grad_in, grad_down)
+    input_grad = reorder((dresid + dinput_norm).astype(jnp.bfloat16))
+    gain_shares = scatter_gains(jnp.stack([grad_gain_attn, grad_gain_mlp]))
     return (
         block_output,
         input_grad,
-        shares[0],
-        shares[1],
-        shares[2],
-        shares[3],
-        shares[4],
-        shares[5],
+        gain_shares[0],
+        grad_qkv,
+        grad_out,
+        gain_shares[1],
+        grad_in,
+        grad_down,
     )
 
 

time: 1270 us -> 729 us (0.57)
  waiting for transfers between devices: 962 us -> 234 us
  local copies, waits for them, and re-layouts: 46.5 us -> 143 us
  starting transfers between devices: 12.1 us -> 95.9 us
  blocking collectives: 83.2 us -> 0 us
  other arithmetic: 32 us -> 99.3 us
  matrix products: 118 us -> 140 us
    reduce_scatter x3 -> x0, waiting for transfers between devices: 625 us -> none  [the longest x1 464 us: scatter_grads(): lax.psum_scatter(w_in, ('seq', 'wt'), scatter_dimension=0, tiled=True)]
    ppermute x0 -> x83, waiting for transfers between devices: none -> 222 us  [swapped(): return lax.ppermute(block, ('seq', 'wt'), route)]
    all_gather x4 -> x0, waiting for transfers between devices: 179 us -> none  [the longest x1 86.8 us: gather_weights(): lax.all_gather(w_in, ('seq', 'wt'), axis=0, tiled=True)]
    unnamed x9 -> x0, waiting for transfers between devices: 126 us -> none
    ppermute x0 -> x83, starting transfers between devices: none -> 86.5 us  [swapped(): return lax.ppermute(block, ('seq', 'wt'), route)]
    unnamed x2 -> x0, blocking collectives: 83.2 us -> none
    concatenate x0 -> x21, other arithmetic: none -> 45.6 us  [the longest x18 43.8 us: gather_rel(): held = jnp.concatenate([held, swapped(held, bit)], axis=axis)]
    slice x0 -> x36, local copies, waits for them, and re-layouts: none -> 39.7 us  [the longest x6 29 us: part(): piece = lax.slice_in_dim(piece, second, second + 1, axis=second_axis)]
  transfers between devices with their start and end apart: 12 -> 87, of which waited for: 11 -> 34; matrix products, arithmetic and copies ran while one was open for 13% -> 40% of each run, Pallas kernels for 0% -> 0%
where the time goes in v1:
time: 729 us; the launch traced here: 716 us
  waiting for transfers between devices  234 us (32%)
  local copies, waits for them, and re-layouts  143 us (20%)
  matrix products  140 us (19%)
  other arithmetic  99.3 us (14%)
  starting transfers between devices  95.9 us (13%)
    ppermute x83, waiting for transfers between devices, swapped(): return lax.ppermute(block, ('seq', 'wt'), route)  222 us
    ppermute x83, starting transfers between devices, swapped(): return lax.ppermute(block, ('seq', 'wt'), route)  86.5 us
    concatenate x18, other arithmetic, gather_rel(): held = jnp.concatenate([held, swapped(held, bit)], axis=axis)  43.8 us
    dot_general x24, matrix products, product(): lax.dot_general(part(core, second), right, (((0,), (0,)), ((), ())), pref...  40.4 us
    slice x6, local copies, waits for them, and re-layouts, part(): piece = lax.slice_in_dim(piece, second, second + 1, axis=second_axis)  29 us
    dot_general x8, matrix products, reorder(): jnp.dot(rows, swap, preferred_element_type=jnp.float32).astype(jnp.bfloat16)  26.5 us
    ppermute x9, local copies, waits for them, and re-layouts, swapped(): return lax.ppermute(block, ('seq', 'wt'), route)  23.5 us
    concatenate x6, local copies, waits for them, and re-layouts, gather_rel(): held = jnp.concatenate([held, swapped(held, bit)], axis=axis)  20.8 us
  transfers between devices with their start and end apart: 87, of which 34 were waited for; matrix products, arithmetic and copies ran while one was open for 40% of the time, Pallas kernels for 0%

profile of v1, /device:TPU:0, one launch (start us, length us, event | category | flops | bytes accessed | tf_op | source)
XLA Modules:
  0.0 715.6 jit_solution(10373260657395228075)
XLA Ops:
  33.0 6.9 collective-permute-done.7
  52.7 6.4 collective-permute-done.21
  59.1 11.5 %collective-permute-start.33 = (bf16[32,2624]{1,0:T(8,128)(2,1)S(1)}, bf16[32,2624]{1,0:T(8,128)(2,1)}, u32[]{:S(2)}, u32[]{:S(2)}) collective-permute-start(bf16[32,2624]{1,0:T(8,128)(2,1)S(1)} %copy-done.103), channel_id=1, source_target_pairs={{0,2},{1,3},{2,0},{3,1},{4,6},{5,7},{6,4},{7,5},{8,10},{9,11},{10,... | collective-permute-start | bytes 503816 | tf_op jit(solution)/shard_map/ppermute | solution.py:70
  97.8 8.6 %collective-permute-done.23 = bf16[1,1,1,128,2624]{3,4,2,1,0:T(8,128)(2,1)} collective-permute-done((bf16[1,1,1,128,2624]{3,4,2,1,0:T(8,128)(2,1)}, bf16[1,1,1,128,2624]{3,4,2,1,0:T(8,128)(2,1)}, u32[]{:S(2)}, u32[]{:S(2)}) %collective-permute-start.23) | collective-permute-done | bytes 671776 | tf_op jit(solution)/shard_map/ppermute | solution.py:70
  115.3 15.1 %collective-permute-done.18 = bf16[1,2,1,128,1024]{4,3,2,1,0:T(8,128)(2,1)} collective-permute-done((bf16[1,2,1,128,1024]{4,3,2,1,0:T(8,128)(2,1)}, bf16[1,2,1,128,1024]{4,3,2,1,0:T(8,128)(2,1)}, u32[]{:S(2)}, u32[]{:S(2)}) %collective-permute-start.18) | collective-permute-done | bytes 524320 | tf_op jit(solution)/shard_map/ppermute | solution.py:70
  157.3 15.9 %collective-permute-done.24 = bf16[1,2,1,128,2624]{3,4,2,1,0:T(8,128)(2,1)} collective-permute-done((bf16[1,2,1,128,2624]{3,4,2,1,0:T(8,128)(2,1)}, bf16[1,2,1,128,2624]{3,4,2,1,0:T(8,128)(2,1)}, u32[]{:S(2)}, u32[]{:S(2)}) %collective-permute-start.24) | collective-permute-done | bytes 1343520 | tf_op jit(solution)/shard_map/ppermute | solution.py:70
  267.6 8.8 %fusion.194 = (f32[16,320]{1,0:T(8,128)S(1)}, f32[16,320,448]{2,1,0:T(8,128)}) fusion(pred[320,448]{1,0:T(8,128)(4,1)S(1)} %copy-done.104, bf16[320,16,64]{0,2,1:T(8,128)(2,1)} %get-tuple-element.172, bf16[448,16,64]{0,2,1:T(8,128)(2,1)S(1)} %bitcast.383), kind=kOutput, calls=%fused_computation.377 | convolution fusion | flops 302776768 | bytes 10911744 | tf_op jit(solution)/shard_map/while/body/eval_jaxpr/sub | solution.py:166
  342.5 13.3 %add_convert_fusion = (bf16[320,2624]{1,0:T(8,128)(2,1)S(1)}, f32[320,2624]{1,0:T(8,128)}, f32[320,2624]{1,0:T(8,128)}) fusion(f32[320,2624]{1,0:T(8,128)} %fusion.198, f32[320,2624]{1,0:T(8,128)S(1)} %copy-done.59, bf16[1024,320]{0,1:T(8,128)(2,1)S(1)} %copy-done.69, bf16[1024,2624]{1,0:T(8,128)(2,1)S(1)} %bitcast.368), kind=kOutput, calls=%fused_computation.37 | convolution fusion | flops 1780961280 | bytes 21143552 | tf_op jit(solution)/shard_map/dot_general | solution.py:253
  355.8 6.3 multiply_convert_fusion.1
  381.0 7.2 %multiply_reduce_fusion = (f32[16,320]{1,0:T(8,128)S(1)}, f32[16,320,448]{2,1,0:T(8,128)S(1)}) fusion(f32[16,320,448]{2,1,0:T(8,128)} %get-tuple-element.183, f32[16,320]{1,0:T(8,128)S(1)} %get-tuple-element.182, bf16[320,16,64]{0,2,1:T(8,128)(2,1)} %bitcast.398, bf16[448,16,64]{0,2,1:T(8,128)(2,1)} %bitcast.397), kind=kOutput, calls=%fused_computation.2 | convolution fusion | flops 300477440 | bytes 19963904 | tf_op jit(solution)/shard_map/while/body/eval_jaxpr/qhd,khd->hqk/dot_general | solution.py:275
  402.7 6.6 fusion.59
  457.6 6.3 scatter-add.6
  463.8 6.2 collective-permute-done.39
  506.6 9.8 %collective-permute-done.61 = bf16[256,1024]{1,0:T(8,128)(2,1)S(1)} collective-permute-done((bf16[256,1024]{1,0:T(8,128)(2,1)S(1)}, bf16[256,1024]{1,0:T(8,128)(2,1)S(1)}, u32[]{:S(2)}, u32[]{:S(2)}) %collective-permute-start.61) | collective-permute-done | bytes 524320 | tf_op jit(solution)/shard_map/ppermute | solution.py:70
  519.8 7.6 %collective-permute-done.62 = bf16[1,4,32,1024]{3,2,1,0:T(8,128)(2,1)S(1)} collective-permute-done((bf16[1,4,32,1024]{3,2,1,0:T(8,128)(2,1)S(1)}, bf16[1,4,32,1024]{3,2,1,0:T(8,128)(2,1)S(1)}, u32[]{:S(2)}, u32[]{:S(2)}) %collective-permute-start.62) | collective-permute-done | bytes 262176 | tf_op jit(solution)/shard_map/ppermute | solution.py:70
  547.2 13.4 %collective-permute-done.54 = bf16[256,1536]{1,0:T(8,128)(2,1)S(1)} collective-permute-done((bf16[256,1536]{1,0:T(8,128)(2,1)S(1)}, bf16[256,1536]{1,0:T(8,128)(2,1)S(1)}, u32[]{:S(2)}, u32[]{:S(2)}) %collective-permute-start.54) | collective-permute-done | bytes 786464 | tf_op jit(solution)/shard_map/ppermute | solution.py:70
  562.8 33.1 %collective-permute-done.48 = bf16[1,4,32,1536]{3,2,1,0:T(8,128)(2,1)S(1)} collective-permute-done((bf16[1,4,32,1536]{3,2,1,0:T(8,128)(2,1)S(1)}, bf16[1,4,32,1536]{3,2,1,0:T(8,128)(2,1)S(1)}, u32[]{:S(2)}, u32[]{:S(2)}) %collective-permute-start.48) | collective-permute-done | bytes 393248 | tf_op jit(solution)/shard_map/ppermute | solution.py:70
  601.9 6.1 collective-permute-done.50
  608.4 6.3 collective-permute-done.57
  619.6 26.9 %collective-permute-done.68 = bf16[256,2624]{0,1:T(8,128)(2,1)S(1)} collective-permute-done((bf16[256,2624]{0,1:T(8,128)(2,1)S(1)}, bf16[256,2624]{0,1:T(8,128)(2,1)S(1)}, u32[]{:S(2)}, u32[]{:S(2)}) %collective-permute-start.68) | collective-permute-done | bytes 1343520 | tf_op jit(solution)/shard_map/ppermute | solution.py:70
  663.3 6.2 collective-permute-done.83
  671.5 7.1 collective-permute-done.69
  687.4 8.7 %collective-permute-done.71 = bf16[32,2624]{1,0:T(8,128)(2,1)S(1)} collective-permute-done((bf16[32,2624]{1,0:T(8,128)(2,1)S(1)}, bf16[32,2624]{1,0:T(8,128)(2,1)S(1)}, u32[]{:S(2)}, u32[]{:S(2)}) %collective-permute-start.71) | collective-permute-done | bytes 167968 | tf_op jit(solution)/shard_map/ppermute | solution.py:70
  700.1 13.2 %collective-permute-done.78 = bf16[32,2624]{1,0:T(8,128)(2,1)S(1)} collective-permute-done((bf16[32,2624]{1,0:T(8,128)(2,1)S(1)}, bf16[32,2624]{1,0:T(8,128)(2,1)S(1)}, u32[]{:S(2)}, u32[]{:S(2)}) %collective-permute-start.78) | collective-permute-done | bytes 167968 | tf_op jit(solution)/shard_map/ppermute | solution.py:70
  (651 shorter events, 454.9 us)
Async XLA Ops:
  2.5 43.0 %collective-permute-start = (bf16[32,1664]{1,0:T(8,128)(2,1)S(1)}, bf16[32,1664]{1,0:T(8,128)(2,1)S(1)}, u32[]{:S(2)}, u32[]{:S(2)}) collective-permute-start(bf16[32,1664]{1,0:T(8,128)(2,1)S(1)} %pad_maximum_fusion.28), channel_id=1, source_target_pairs={{0,1},{1,0},{2,3},{3,2},{4,5},{5,4},{6,7},{7,6},{8,9},{9,8},{10,11... | collective-permute-start | bytes 319496 | tf_op jit(solution)/shard_map/ppermute | solution.py:70
  5.6 41.6 %collective-permute-start.1 = (bf16[32,1664]{1,0:T(8,128)(2,1)S(1)}, bf16[32,1664]{1,0:T(8,128)(2,1)S(1)}, u32[]{:S(2)}, u32[]{:S(2)}) collective-permute-start(bf16[32,1664]{1,0:T(8,128)(2,1)S(1)} %pad_maximum_fusion.28), channel_id=1, source_target_pairs={{0,2},{1,3},{2,0},{3,1},{4,6},{5,7},{6,4},{7,5},{8,10},{9,11},{10,... | collective-permute-start | bytes 319496 | tf_op jit(solution)/shard_map/ppermute | solution.py:70
  90.4 46.0 %collective-permute-start.35 = (bf16[1,1,1,128,2624]{3,4,2,1,0:T(8,128)(2,1)}, bf16[1,1,1,128,2624]{3,4,2,1,0:T(8,128)(2,1)}, u32[]{:S(2)}, u32[]{:S(2)}) collective-permute-start(bf16[1,1,1,128,2624]{3,4,2,1,0:T(8,128)(2,1)} %copy.198), channel_id=1, source_target_pairs={{0,16},{1,17},{2,18},{3,19},{4,20},{5,21},{6,22},{7,23},{8,24},{9,... | collective-permute-start | bytes 2015240 | tf_op jit(solution)/shard_map/ppermute | solution.py:70
  91.7 38.7 %collective-permute-start.18 = (bf16[1,2,1,128,1024]{4,3,2,1,0:T(8,128)(2,1)}, bf16[1,2,1,128,1024]{4,3,2,1,0:T(8,128)(2,1)}, u32[]{:S(2)}, u32[]{:S(2)}) collective-permute-start(bf16[1,2,1,128,1024]{4,3,2,1,0:T(8,128)(2,1)} %pad_maximum_fusion.24), channel_id=1, source_target_pairs={{0,16},{1,17},{2,18},{3,19},{4,20},{5,21},{6,22},{7,23},{8,24},{9,... | collective-permute-start | bytes 1572872 | tf_op jit(solution)/shard_map/ppermute | solution.py:70
  95.2 46.8 %collective-permute-start.10 = (bf16[2,1,1,128,1536]{4,3,2,1,0:T(8,128)(2,1)}, bf16[2,1,1,128,1536]{4,3,2,1,0:T(8,128)(2,1)}, u32[]{:S(2)}, u32[]{:S(2)}) collective-permute-start(bf16[2,1,1,128,1536]{4,3,2,1,0:T(8,128)(2,1)} %pad_maximum_fusion.22), channel_id=1, source_target_pairs={{0,8},{1,9},{2,10},{3,11},{4,12},{5,13},{6,14},{7,15},{8,0},{9,1},... | collective-permute-start | bytes 2359304 | tf_op jit(solution)/shard_map/ppermute | solution.py:70
  106.4 42.3 %collective-permute-start.4 = (bf16[1,2,1,128,1664]{4,3,2,1,0:T(8,128)(2,1)}, bf16[1,2,1,128,1664]{4,3,2,1,0:T(8,128)(2,1)}, u32[]{:S(2)}, u32[]{:S(2)}) collective-permute-start(bf16[1,2,1,128,1664]{4,3,2,1,0:T(8,128)(2,1)} %pad_maximum_fusion.21), channel_id=1, source_target_pairs={{0,16},{1,17},{2,18},{3,19},{4,20},{5,21},{6,22},{7,23},{8,24},{9,... | collective-permute-start | bytes 2555912 | tf_op jit(solution)/shard_map/ppermute | solution.py:70
  113.7 59.5 %collective-permute-start.24 = (bf16[1,2,1,128,2624]{3,4,2,1,0:T(8,128)(2,1)}, bf16[1,2,1,128,2624]{3,4,2,1,0:T(8,128)(2,1)}, u32[]{:S(2)}, u32[]{:S(2)}) collective-permute-start(bf16[1,2,1,128,2624]{3,4,2,1,0:T(8,128)(2,1)} %copy.188), channel_id=1, source_target_pairs={{0,16},{1,17},{2,18},{3,19},{4,20},{5,21},{6,22},{7,23},{8,24},{9,... | collective-permute-start | bytes 4030472 | tf_op jit(solution)/shard_map/ppermute | solution.py:70
  136.3 46.6 %collective-permute-start.30 = (bf16[2,1,1,128,2624]{3,4,2,1,0:T(8,128)(2,1)}, bf16[2,1,1,128,2624]{3,4,2,1,0:T(8,128)(2,1)}, u32[]{:S(2)}, u32[]{:S(2)}) collective-permute-start(bf16[2,1,1,128,2624]{3,4,2,1,0:T(8,128)(2,1)} %copy.194), channel_id=1, source_target_pairs={{0,8},{1,9},{2,10},{3,11},{4,12},{5,13},{6,14},{7,15},{8,0},{9,1},... | collective-permute-start | bytes 4030472 | tf_op jit(solution)/shard_map/ppermute | solution.py:70
  142.1 55.3 %collective-permute-start.36 = (bf16[2,1,1,128,2624]{3,4,2,1,0:T(8,128)(2,1)}, bf16[2,1,1,128,2624]{3,4,2,1,0:T(8,128)(2,1)}, u32[]{:S(2)}, u32[]{:S(2)}) collective-permute-start(bf16[2,1,1,128,2624]{3,4,2,1,0:T(8,128)(2,1)} %copy.200), channel_id=1, source_target_pairs={{0,8},{1,9},{2,10},{3,11},{4,12},{5,13},{6,14},{7,15},{8,0},{9,1},... | collective-permute-start | bytes 4030472 | tf_op jit(solution)/shard_map/ppermute | solution.py:70
  148.7 58.4 %collective-permute-start.11 = (bf16[2,2,1,128,1536]{4,3,2,1,0:T(8,128)(2,1)}, bf16[2,2,1,128,1536]{4,3,2,1,0:T(8,128)(2,1)}, u32[]{:S(2)}, u32[]{:S(2)}) collective-permute-start(bf16[2,2,1,128,1536]{4,3,2,1,0:T(8,128)(2,1)} %pad_maximum_fusion.12), channel_id=1, source_target_pairs={{0,4},{1,5},{2,6},{3,7},{4,0},{5,1},{6,2},{7,3},{8,12},{9,13},{10,... | collective-permute-start | bytes 4718600 | tf_op jit(solution)/shard_map/ppermute | solution.py:70
  151.4 58.9 %collective-permute-start.5 = (bf16[2,2,1,128,1664]{4,3,2,1,0:T(8,128)(2,1)}, bf16[2,2,1,128,1664]{4,3,2,1,0:T(8,128)(2,1)}, u32[]{:S(2)}, u32[]{:S(2)}) collective-permute-start(bf16[2,2,1,128,1664]{4,3,2,1,0:T(8,128)(2,1)} %pad_maximum_fusion.11), channel_id=1, source_target_pairs={{0,4},{1,5},{2,6},{3,7},{4,0},{5,1},{6,2},{7,3},{8,12},{9,13},{10,... | collective-permute-start | bytes 5111816 | tf_op jit(solution)/shard_map/ppermute | solution.py:70
  183.0 125.8 %collective-permute-start.25 = (bf16[2,2,1,128,2624]{3,4,2,1,0:T(8,128)(2,1)}, bf16[2,2,1,128,2624]{3,4,2,1,0:T(8,128)(2,1)}, u32[]{:S(2)}, u32[]{:S(2)}) collective-permute-start(bf16[2,2,1,128,2624]{3,4,2,1,0:T(8,128)(2,1)} %copy.190), channel_id=1, source_target_pairs={{0,4},{1,5},{2,6},{3,7},{4,0},{5,1},{6,2},{7,3},{8,12},{9,13},{10,... | collective-permute-start | bytes 8060936 | tf_op jit(solution)/shard_map/ppermute | solution.py:70
  192.7 120.6 %collective-permute-start.31 = (bf16[2,2,1,128,2624]{3,4,2,1,0:T(8,128)(2,1)}, bf16[2,2,1,128,2624]{3,4,2,1,0:T(8,128)(2,1)}, u32[]{:S(2)}, u32[]{:S(2)}) collective-permute-start(bf16[2,2,1,128,2624]{3,4,2,1,0:T(8,128)(2,1)} %copy.196), channel_id=1, source_target_pairs={{0,4},{1,5},{2,6},{3,7},{4,0},{5,1},{6,2},{7,3},{8,12},{9,13},{10,... | collective-permute-start | bytes 8060936 | tf_op jit(solution)/shard_map/ppermute | solution.py:70
  207.1 126.1 %collective-permute-start.37 = (bf16[2,2,1,128,2624]{3,4,2,1,0:T(8,128)(2,1)}, bf16[2,2,1,128,2624]{3,4,2,1,0:T(8,128)(2,1)}, u32[]{:S(2)}, u32[]{:S(2)}) collective-permute-start(bf16[2,2,1,128,2624]{3,4,2,1,0:T(8,128)(2,1)} %copy.202), channel_id=1, source_target_pairs={{0,4},{1,5},{2,6},{3,7},{4,0},{5,1},{6,2},{7,3},{8,12},{9,13},{10,... | collective-permute-start | bytes 8060936 | tf_op jit(solution)/shard_map/ppermute | solution.py:70
  412.4 115.4 %collective-permute-start.81 = (bf16[256,2624]{0,1:T(8,128)(2,1)}, bf16[256,2624]{0,1:T(8,128)(2,1)}, u32[]{:S(2)}, u32[]{:S(2)}) collective-permute-start(bf16[256,2624]{0,1:T(8,128)(2,1)} %convolution_convert_fusion), channel_id=1, source_target_pairs={{0,4},{1,5},{2,6},{3,7},{4,0},{5,1},{6,2},{7,3},{8,12},{9,13},{10,... | collective-permute-start | bytes 4030472 | tf_op jit(solution)/shard_map/ppermute | solution.py:70
  433.0 68.9 %collective-permute-start.60 = (bf16[256,1024]{1,0:T(8,128)(2,1)}, bf16[256,1024]{1,0:T(8,128)(2,1)}, u32[]{:S(2)}, u32[]{:S(2)}) collective-permute-start(bf16[256,1024]{1,0:T(8,128)(2,1)} %convolution_convert_fusion.11), channel_id=1, source_target_pairs={{0,4},{1,5},{2,6},{3,7},{4,0},{5,1},{6,2},{7,3},{8,12},{9,13},{10,... | collective-permute-start | bytes 1572872 | tf_op jit(solution)/shard_map/ppermute | solution.py:70
  434.3 71.7 %collective-permute-start.59 = (bf16[256,1024]{1,0:T(8,128)(2,1)}, bf16[256,1024]{1,0:T(8,128)(2,1)}, u32[]{:S(2)}, u32[]{:S(2)}) collective-permute-start(bf16[256,1024]{1,0:T(8,128)(2,1)} %convolution_convert_fusion.12), channel_id=1, source_target_pairs={{0,4},{1,5},{2,6},{3,7},{4,0},{5,1},{6,2},{7,3},{8,12},{9,13},{10,... | collective-permute-start | bytes 1572872 | tf_op jit(solution)/shard_map/ppermute | solution.py:70
  538.4 78.8 %collective-permute-start.80 = (bf16[256,2624]{0,1:T(8,128)(2,1)S(1)}, bf16[256,2624]{0,1:T(8,128)(2,1)S(1)}, u32[]{:S(2)}, u32[]{:S(2)}) collective-permute-start(bf16[256,2624]{0,1:T(8,128)(2,1)S(1)} %copy-done.76), channel_id=1, source_target_pairs={{0,4},{1,5},{2,6},{3,7},{4,0},{5,1},{6,2},{7,3},{8,12},{9,13},{10,... | collective-permute-start | bytes 4030472 | tf_op jit(solution)/shard_map/ppermute | solution.py:70
  541.4 76.1 %collective-permute-start.82 = (bf16[256,2624]{0,1:T(8,128)(2,1)S(1)}, bf16[256,2624]{0,1:T(8,128)(2,1)S(1)}, u32[]{:S(2)}, u32[]{:S(2)}) collective-permute-start(bf16[256,2624]{0,1:T(8,128)(2,1)S(1)} %add_convert_fusion.1), channel_id=1, source_target_pairs={{0,16},{1,17},{2,18},{3,19},{4,20},{5,21},{6,22},{7,23},{8,24},{9,... | collective-permute-start | bytes 4030472 | tf_op jit(solution)/shard_map/ppermute | solution.py:70
  546.5 49.3 %collective-permute-start.48 = (bf16[1,4,32,1536]{3,2,1,0:T(8,128)(2,1)S(1)}, bf16[1,4,32,1536]{3,2,1,0:T(8,128)(2,1)S(1)}, u32[]{:S(2)}, u32[]{:S(2)}) collective-permute-start(bf16[1,4,32,1536]{3,2,1,0:T(8,128)(2,1)S(1)} %bitcast.421), channel_id=1, source_target_pairs={{0,16},{1,17},{2,18},{3,19},{4,20},{5,21},{6,22},{7,23},{8,24},{9,... | collective-permute-start | bytes 1179656 | tf_op jit(solution)/shard_map/ppermute | solution.py:70
  561.0 37.0 %collective-permute-start.55 = (bf16[1,4,32,1536]{3,2,1,0:T(8,128)(2,1)S(1)}, bf16[1,4,32,1536]{3,2,1,0:T(8,128)(2,1)S(1)}, u32[]{:S(2)}, u32[]{:S(2)}) collective-permute-start(bf16[1,4,32,1536]{3,2,1,0:T(8,128)(2,1)S(1)} %bitcast.420), channel_id=1, source_target_pairs={{0,8},{1,9},{2,10},{3,11},{4,12},{5,13},{6,14},{7,15},{8,0},{9,1},... | collective-permute-start | bytes 1179656 | tf_op jit(solution)/shard_map/ppermute | solution.py:70
  614.6 38.0 %collective-permute-start.73 = (bf16[256,2624]{0,1:T(8,128)(2,1)}, bf16[256,2624]{0,1:T(8,128)(2,1)}, u32[]{:S(2)}, u32[]{:S(2)}) collective-permute-start(bf16[256,2624]{0,1:T(8,128)(2,1)} %convolution_convert_fusion.3), channel_id=1, source_target_pairs={{0,4},{1,5},{2,6},{3,7},{4,0},{5,1},{6,2},{7,3},{8,12},{9,13},{10,... | collective-permute-start | bytes 4030472 | tf_op jit(solution)/shard_map/ppermute | solution.py:70
  671.4 43.0 %collective-permute-start.84 = (bf16[32,2624]{1,0:T(8,128)(2,1)S(1)}, bf16[32,2624]{1,0:T(8,128)(2,1)S(1)}, u32[]{:S(2)}, u32[]{:S(2)}) collective-permute-start(bf16[32,2624]{1,0:T(8,128)(2,1)S(1)} %get-tuple-element.150), channel_id=1, source_target_pairs={{0,1},{1,0},{2,3},{3,2},{4,5},{5,4},{6,7},{7,6},{8,9},{9,8},{10,11... | collective-permute-start | bytes 503816 | tf_op jit(solution)/shard_map/ppermute | solution.py:70
  671.4 43.0 %collective-permute-start.85 = (bf16[32,2624]{1,0:T(8,128)(2,1)S(1)}, bf16[32,2624]{1,0:T(8,128)(2,1)S(1)}, u32[]{:S(2)}, u32[]{:S(2)}) collective-permute-start(bf16[32,2624]{1,0:T(8,128)(2,1)S(1)} %get-tuple-element.152), channel_id=1, source_target_pairs={{0,2},{1,3},{2,0},{3,1},{4,6},{5,7},{6,4},{7,5},{8,10},{9,11},{10,... | collective-permute-start | bytes 503816 | tf_op jit(solution)/shard_map/ppermute | solution.py:70
  (203 other events, 2474.2 us)

commit v2 on v1

--- a/solution.py
+++ b/solution.py
@@ -70,63 +70,72 @@
     return lax.ppermute(block, ("seq", "wt"), route)
 
 
-def stage_bits(flip):
+def far_bits():
     near = lax.axis_size("wt")
     far = []
     bit = near
     while bit < device_count():
         far.append(bit)
         bit *= 2
-    first, rest = far[0], far[1:]
-    return near, first, rest[::-1] if flip else rest
+    return near, far[0], far[:0:-1]
+
+
+def block_masks():
+    near, first, rest = far_bits()
+    masks = [0]
+    for bit in [first] + rest:
+        masks = [mask | extra for mask in masks for extra in (0, bit)]
+    return [mask | j for mask in masks for j in range(near)]
 
 
 def gather_rel(block, flip):
-    near, first, rest = stage_bits(flip)
-    levels = len(rest) + 1
+    near, first, rest = far_bits()
+    levels = len(rest)
     held = jnp.concatenate([block] + [swapped(block, j) for j in range(1, near)], axis=0)
     held = held.reshape((1,) * levels + held.shape)
-    for bit in rest + [first]:
-        axis = levels - 1 - ((bit // near).bit_length() - 1)
-        held = jnp.concatenate([held, swapped(held, bit)], axis=axis)
-    return held.reshape(-1, block.shape[1])
-
-
-def scatter_rel(left, right, flip):
-    near, first, rest = stage_bits(flip)
-    rows = left.shape[1] // device_count()
-    levels = len(rest) + 1
-    tokens = left.shape[0]
-    parts = left.reshape((tokens,) + (2,) * levels + (near * rows,))
-    first_axis = levels
-    second_axis = levels - ((rest[0] // near).bit_length() - 1)
-
-    def part(core, second):
-        piece = lax.slice_in_dim(parts, core, core + 1, axis=first_axis)
-        piece = lax.slice_in_dim(piece, second, second + 1, axis=second_axis)
-        return piece.reshape(tokens, -1)
+    for bit in rest if flip else rest[::-1]:
+        held = jnp.concatenate([held, swapped(held, bit)], axis=rest.index(bit))
+    held = held.reshape(-1, block.shape[1])
+    return held, swapped(held, first)
+
+
+def scatter_begin(left, right, flip):
+    near, first, rest = far_bits()
+    width = left.shape[1]
+    unit = width // (2 ** (len(rest) + 1))
+    top = rest[0] if flip else rest[-1]
+    place = len(rest) - 1 - rest.index(top)
 
     def product(core, second):
+        base = core * width // 2
+        picked = [k for k in range(2 ** len(rest)) if (k >> place) & 1 == second]
+        part = jnp.concatenate(
+            [left[:, base + k * unit : base + (k + 1) * unit] for k in picked], axis=1
+        )
         return lax.dot_general(
-            part(core, second),
-            right,
-            (((0,), (0,)), ((), ())),
-            preferred_element_type=jnp.float32,
+            part, right, (((0,), (0,)), ((), ())), preferred_element_type=jnp.float32
         )
 
     got_far = swapped(product(1, 1).astype(jnp.bfloat16), first)
     got_near = swapped(product(1, 0).astype(jnp.bfloat16), first)
     far = (product(0, 1) + got_far.astype(jnp.float32)).astype(jnp.bfloat16)
-    got = swapped(far, rest[0])
-    total = product(0, 0) + got_near.astype(jnp.float32) + got.astype(jnp.float32)
-    remaining = sorted(rest[1:], reverse=True)
-    total = total.reshape((2,) * len(remaining) + (near, rows, right.shape[1]))
-    for bit in rest[1:]:
-        axis = remaining.index(bit)
+    kept = product(0, 0) + got_near.astype(jnp.float32)
+    return kept, swapped(far, top)
+
+
+def scatter_end(begun, flip):
+    near, first, rest = far_bits()
+    kept, got = begun
+    top = rest[0] if flip else rest[-1]
+    total = kept + got.astype(jnp.float32)
+    remaining = [bit for bit in rest if bit != top]
+    rows = 2 * kept.shape[0] // (device_count() // 2)
+    total = total.reshape((2,) * len(remaining) + (near, rows, kept.shape[1]))
+    for axis, bit in enumerate(remaining):
         keep = lax.slice_in_dim(total, 0, 1, axis=axis)
         send = lax.slice_in_dim(total, 1, 2, axis=axis).astype(jnp.bfloat16)
         total = keep + swapped(send, bit).astype(jnp.float32)
-    total = total.reshape(near, rows, right.shape[1])
+    total = total.reshape(near, rows, kept.shape[1])
     result = total[0]
     for j in range(1, near):
         result = result + swapped(total[j].astype(jnp.bfloat16), j).astype(jnp.float32)
@@ -134,11 +143,30 @@
 
 
 def scatter_gains(gains):
+    near, first, rest = far_bits()
     total = gains.reshape(gains.shape[0], device_count(), -1).swapaxes(0, 1)
-    while total.shape[0] > 1:
+    bits = [first] + rest
+    while near > 1:
+        near //= 2
+        bits.append(near)
+    for bit in bits:
         half = total.shape[0] // 2
-        total = total[:half] + swapped(total[half:], half)
+        total = total[:half] + swapped(total[half:], bit)
     return total[0]
+
+
+def times(rows, halves):
+    middle = rows.shape[1] // 2
+    return jnp.dot(
+        rows[:, :middle], halves[0], preferred_element_type=jnp.float32
+    ) + jnp.dot(rows[:, middle:], halves[1], preferred_element_type=jnp.float32)
+
+
+def times_transposed(rows, halves):
+    return jnp.concatenate(
+        [jnp.einsum("tf,df->td", rows, h, preferred_element_type=jnp.float32) for h in halves],
+        axis=1,
+    )
 
 
 def block_mask(positions, block_start, block_rows, token_total, at_first, at_last):
@@ -180,20 +208,31 @@
     gains = jnp.pad(gains, ((0, 0), (0, 126)))
     full_one = gather_rel(jnp.concatenate([w_qkv[:, :cut], gains], axis=1), False)
     full_two = gather_rel(w_qkv[:, cut:], True)
+    w_out, w_in, one, two = lax.optimization_barrier((w_out, w_in, full_one[0], full_two[0]))
+    full_one, full_two = (one, full_one[1]), (two, full_two[1])
     full_out = gather_rel(w_out, False)
     full_first = gather_rel(w_in[:, :hidden_units], False)
     full_second = gather_rel(w_in[:, hidden_units:], True)
+    w_down, one, two = lax.optimization_barrier((w_down, full_first[0], full_second[0]))
+    full_first, full_second = (one, full_first[1]), (two, full_second[1])
     full_down = gather_rel(w_down, True)
-    gain_attn = full_one[:, cut]
-    gain_mlp = full_one[:, cut + 1]
-    full_one = full_one[:, :cut]
-    order = jnp.arange(width, dtype=jnp.int32) ^ (device_index * w_out.shape[0])
-    swap = (order[:, None] == jnp.arange(width, dtype=jnp.int32)[None, :]).astype(jnp.bfloat16)
+    gathered = jnp.concatenate([half[:, cut : cut + 2] for half in full_one], axis=0)
+    gain_attn, gain_mlp = gathered[:, 0], gathered[:, 1]
+    full_one = [half[:, :cut] for half in full_one]
+    rows = w_out.shape[0]
+    masks = jnp.repeat(jnp.array(block_masks(), dtype=jnp.int32), rows) * rows
+    columns = jnp.arange(width, dtype=jnp.int32)
+    source = (masks + columns % rows) ^ (device_index * rows)
+    swap = (columns[:, None] == source[None, :]).astype(jnp.bfloat16)
 
     def reorder(rows):
         return jnp.dot(rows, swap, preferred_element_type=jnp.float32).astype(jnp.bfloat16)
 
-    full_out = reorder(full_out)
+    def restore(rows):
+        moved = jnp.einsum("tj,ij->ti", rows, swap, preferred_element_type=jnp.float32)
+        return moved.astype(jnp.bfloat16)
+
+    full_out = [reorder(half) for half in full_out]
     block_input = reorder(block_input)
     cotangent = reorder(cotangent)
     at_first = device_index == 0
@@ -203,8 +242,8 @@
     act_one = normed_one.astype(jnp.bfloat16)
     qkv = jnp.concatenate(
         [
-            jnp.dot(act_one, full_one, preferred_element_type=jnp.float32),
-            jnp.dot(act_one, full_two, preferred_element_type=jnp.float32),
+            times(act_one, full_one),
+            times(act_one, full_two),
         ],
         axis=1,
     )
@@ -240,32 +279,29 @@
 
     mixed, stored = lax.map(forward_block, starts)
     attn = reorder(mixed.reshape(token_total, width).astype(jnp.bfloat16))
-    resid = inputs + jnp.dot(attn, full_out, preferred_element_type=jnp.float32)
+    resid = inputs + times(attn, full_out)
     normed_two, norm_two_back = jax.vjp(layer_norm, resid, gain_mlp.astype(jnp.float32))
     act_two = normed_two.astype(jnp.bfloat16)
-    first = jnp.dot(act_two, full_first, preferred_element_type=jnp.float32)
-    second = jnp.dot(act_two, full_second, preferred_element_type=jnp.float32)
+    first = times(act_two, full_first)
+    second = times(act_two, full_second)
     gated_value, gated_back = jax.vjp(gated, first, second)
     hidden = gated_value.astype(jnp.bfloat16)
-    output = resid + jnp.einsum("tf,df->td", hidden, full_down, preferred_element_type=jnp.float32)
-    block_output = reorder(output.astype(jnp.bfloat16))
-    grad_down = scatter_rel(cotangent, hidden, True)
-    dhidden = jnp.dot(cotangent, full_down, preferred_element_type=jnp.float32)
+    output = resid + times_transposed(hidden, full_down)
+    block_output = restore(output.astype(jnp.bfloat16))
+    begun_down = scatter_begin(cotangent, hidden, True)
+    dhidden = times(cotangent, full_down)
     dfirst, dsecond = gated_back(dhidden)
     dfirst = dfirst.astype(jnp.bfloat16)
     dsecond = dsecond.astype(jnp.bfloat16)
-    grad_in = jnp.concatenate(
-        [scatter_rel(act_two, dfirst, False), scatter_rel(act_two, dsecond, True)], axis=1
-    )
-    dact_two = jnp.einsum(
-        "tf,df->td", dfirst, full_first, preferred_element_type=jnp.float32
-    ) + jnp.einsum("tf,df->td", dsecond, full_second, preferred_element_type=jnp.float32)
+    begun_first = scatter_begin(act_two, dfirst, False)
+    begun_second = scatter_begin(act_two, dsecond, True)
+    dact_two = times_transposed(dfirst, full_first) + times_transposed(dsecond, full_second)
     dresid_norm, grad_gain_mlp = norm_two_back(dact_two)
     dresid = cotangent.astype(jnp.float32) + dresid_norm
     dresid_low = dresid.astype(jnp.bfloat16)
-    grad_out = scatter_rel(attn, reorder(dresid_low), False)
-    dattn = jnp.einsum("to,io->ti", dresid_low, full_out, preferred_element_type=jnp.float32)
-    dattn = reorder(dattn.astype(jnp.bfloat16)).reshape(token_total, HEADS, HEAD_DIM)
+    dattn = restore(times_transposed(dresid_low, full_out).astype(jnp.bfloat16))
+    dattn, begun_down = lax.optimization_barrier((dattn, begun_down))
+    dattn = dattn.reshape(token_total, HEADS, HEAD_DIM)
     zeros_ext = jnp.zeros((token_total + 2 * WING, HEADS, HEAD_DIM), jnp.float32)
 
     def backward_block(carry, block_start):
@@ -291,6 +327,14 @@
         return ((key_grad, value_grad), dquery)
 
     (key_grad, value_grad), dquery = lax.scan(backward_block, (zeros_ext, zeros_ext), starts)
+    key_grad, value_grad, dquery, begun_first, begun_second = lax.optimization_barrier(
+        (key_grad, value_grad, dquery, begun_first, begun_second)
+    )
+    grad_down = scatter_end(begun_down, True)
+    grad_in = jnp.concatenate(
+        [scatter_end(begun_first, False), scatter_end(begun_second, True)], axis=1
+    )
+    begun_out = scatter_begin(attn, restore(dresid_low), False)
     edge_grad = jnp.concatenate(
         [key_grad.reshape(-1, width), value_grad.reshape(-1, width)], axis=1
     )
@@ -312,18 +356,17 @@
         ],
         axis=1,
     ).astype(jnp.bfloat16)
+    begun_one = scatter_begin(act_one, dqkv[:, :cut], False)
+    begun_two = scatter_begin(act_one, dqkv[:, cut:], True)
+    grad_out = scatter_end(begun_out, False)
     grad_qkv = jnp.concatenate(
-        [
-            scatter_rel(act_one, dqkv[:, :cut], False),
-            scatter_rel(act_one, dqkv[:, cut:], True),
-        ],
-        axis=1,
-    )
-    dact_one = jnp.einsum(
-        "tf,df->td", dqkv[:, :cut], full_one, preferred_element_type=jnp.float32
-    ) + jnp.einsum("tf,df->td", dqkv[:, cut:], full_two, preferred_element_type=jnp.float32)
+        [scatter_end(begun_one, False), scatter_end(begun_two, True)], axis=1
+    )
+    dact_one = times_transposed(dqkv[:, :cut], full_one) + times_transposed(
+        dqkv[:, cut:], full_two
+    )
     dinput_norm, grad_gain_attn = norm_one_back(dact_one)
-    input_grad = reorder((dresid + dinput_norm).astype(jnp.bfloat16))
+    input_grad = restore((dresid + dinput_norm).astype(jnp.bfloat16))
     gain_shares = scatter_gains(jnp.stack([grad_gain_attn, grad_gain_mlp]))
     return (
         block_output,

time: 729 us -> 610 us (0.84)
  waiting for transfers between devices: 234 us -> 159 us
  starting transfers between devices: 95.9 us -> 121 us
  local copies, waits for them, and re-layouts: 143 us -> 118 us
  other arithmetic: 99.3 us -> 75.7 us
  matrix products: 140 us -> 125 us
    ppermute x83, waiting for transfers between devices: 222 us -> 159 us  [swapped(): return lax.ppermute(block, ('seq', 'wt'), route)]
    ppermute x83, starting transfers between devices: 86.5 us -> 111 us  [swapped(): return lax.ppermute(block, ('seq', 'wt'), route)]
    concatenate x20 -> x14, other arithmetic: 45.6 us -> 21.9 us  [the longest x12 20.2 us: gather_rel(): held = jnp.concatenate([held, swapped(held, bit)], axis=rest.index(bit))]
    slice x35 -> x33, local copies, waits for them, and re-layouts: 38.6 us -> 19.6 us  [the longest x9 9.67 us: scatter_end(): send = lax.slice_in_dim(total, 1, 2, axis=axis).astype(jnp.bfloat16)]
    dot_general x8 -> x5, matrix products: 26.5 us -> 10.8 us  [reorder(): jnp.dot(rows, swap, preferred_element_type=jnp.float32).astype(jnp.bfloat16)]
    concatenate x6 -> x3, local copies, waits for them, and re-layouts: 20.8 us -> 7.53 us  [gather_rel(): held = jnp.concatenate([held, swapped(held, bit)], axis=rest.index(bit))]
    ppermute x2, waiting for transfers between devices: 10 us -> 0.01 us  [shifted(): return lax.ppermute(block, axis, route)]
    ppermute x9 -> x6, local copies, waits for them, and re-layouts: 23.5 us -> 14 us  [swapped(): return lax.ppermute(block, ('seq', 'wt'), route)]
  transfers between devices with their start and end apart: 87 -> 87, of which waited for: 34 -> 33; matrix products, arithmetic and copies ran while one was open for 40% -> 40% of each run, Pallas kernels for 0% -> 0%
where the time goes in v2:
time: 610 us; the launch traced here: 603 us
  waiting for transfers between devices  159 us (26%)
  matrix products  125 us (20%)
  starting transfers between devices  121 us (20%)
  local copies, waits for them, and re-layouts  118 us (19%)
  other arithmetic  75.7 us (12%)
    ppermute x83, waiting for transfers between devices, swapped(): return lax.ppermute(block, ('seq', 'wt'), route)  159 us
    ppermute x83, starting transfers between devices, swapped(): return lax.ppermute(block, ('seq', 'wt'), route)  111 us
    dot_general x24, matrix products, product(): lax.dot_general(part, right, (((0,), (0,)), ((), ())), preferred_element_...  31.9 us
    concatenate x12, other arithmetic, gather_rel(): held = jnp.concatenate([held, swapped(held, bit)], axis=rest.index(bit))  20.2 us
    unnamed x257, local copies, waits for them, and re-layouts  18.1 us
    dot_general x12, matrix products, times_transposed(): jnp.einsum('tf,df->td', rows, h, preferred_element_type=jnp.float32)  17.8 us
    dot_general x6, matrix products, times(): jnp.dot(rows[:, :middle], halves[0], preferred_element_type=jnp.float32)  15.9 us
    reshape x4, local copies, waits for them, and re-layouts, gather_rel(): held = held.reshape(-1, block.shape[1])  15.2 us
  transfers between devices with their start and end apart: 87, of which 33 were waited for; matrix products, arithmetic and copies ran while one was open for 40% of the time, Pallas kernels for 0%

profile of v2, /device:TPU:0, one launch (start us, length us, event | category | flops | bytes accessed | tf_op | source)
XLA Modules:
  0.0 602.6 jit_solution(1804931985998518309)
XLA Ops:
  1.7 5.1 collective-permute-start.7
  31.5 5.5 collective-permute-done.3
  41.5 10.5 %collective-permute-done.9 = bf16[2,1,128,1536]{3,2,1,0:T(8,128)(2,1)S(1)} collective-permute-done((bf16[2,1,128,1536]{3,2,1,0:T(8,128)(2,1)S(1)}, bf16[2,1,128,1536]{3,2,1,0:T(8,128)(2,1)S(1)}, u32[]{:S(2)}, u32[]{:S(2)}) %collective-permute-start.9) | collective-permute-done | bytes 786464 | tf_op jit(solution)/shard_map/ppermute | solution.py:70
  78.3 6.8 %collective-permute-done.21 = bf16[32,2624]{1,0:T(8,128)(2,1)S(1)} collective-permute-done((bf16[32,2624]{1,0:T(8,128)(2,1)S(1)}, bf16[32,2624]{1,0:T(8,128)(2,1)S(1)}, u32[]{:S(2)}, u32[]{:S(2)}) %collective-permute-start.21) | collective-permute-done | bytes 167968 | tf_op jit(solution)/shard_map/ppermute | solution.py:70
  101.8 7.2 %collective-permute-done.23 = bf16[1,1,128,2624]{2,3,1,0:T(8,128)(2,1)} collective-permute-done((bf16[1,1,128,2624]{2,3,1,0:T(8,128)(2,1)}, bf16[1,1,128,2624]{2,3,1,0:T(8,128)(2,1)}, u32[]{:S(2)}, u32[]{:S(2)}) %collective-permute-start.23) | collective-permute-done | bytes 671776 | tf_op jit(solution)/shard_map/ppermute | solution.py:70
  183.9 9.9 %collective-permute-done.33 = bf16[32,2624]{1,0:T(8,128)(2,1)S(1)} collective-permute-done((bf16[32,2624]{1,0:T(8,128)(2,1)S(1)}, bf16[32,2624]{1,0:T(8,128)(2,1)S(1)}, u32[]{:S(2)}, u32[]{:S(2)}) %collective-permute-start.33) | collective-permute-done | bytes 167968 | tf_op jit(solution)/shard_map/ppermute | solution.py:70
  204.8 9.2 %fusion.251 = (f32[16,320]{1,0:T(8,128)S(1)}, f32[16,320,448]{2,1,0:T(8,128)}) fusion(pred[320,448]{1,0:T(8,128)(4,1)} %fusion.89, bf16[320,16,64]{0,2,1:T(8,128)(2,1)} %get-tuple-element.210, bf16[448,16,64]{0,2,1:T(8,128)(2,1)} %bitcast.294), kind=kOutput, calls=%fused_computation.410 | convolution fusion | flops 302776768 | bytes 10911744 | tf_op jit(solution)/shard_map/while/body/eval_jaxpr/sub | solution.py:194
  222.6 6.0 fusion.52
  237.1 5.0 copy.127
  243.0 9.2 %collective-permute-done.36 = bf16[2,1,128,2624]{2,3,1,0:T(8,128)(2,1)} collective-permute-done((bf16[2,1,128,2624]{2,3,1,0:T(8,128)(2,1)}, bf16[2,1,128,2624]{2,3,1,0:T(8,128)(2,1)}, u32[]{:S(2)}, u32[]{:S(2)}) %collective-permute-start.36) | collective-permute-done | bytes 1343520 | tf_op jit(solution)/shard_map/ppermute | solution.py:70
  277.4 10.7 %add_convert_fusion = (bf16[320,2624]{1,0:T(8,128)(2,1)S(1)}, f32[320,2624]{1,0:T(8,128)}, f32[320,2624]{1,0:T(8,128)}) fusion(f32[320,2624]{1,0:T(8,128)S(1)} %convolution_add_fusion.1, f32[320,2624]{1,0:T(8,128)S(1)} %convolution_add_fusion.2, f32[320,2624]{1,0:T(8,128)S(1)} %fusion.99, bf16[512,2624]{1,0:T(8,128)(2,1)S(1)} %bitcast.279, ...), kind=kOutput, calls=%fused_computation.38 | convolution fusion | flops 921968640 | bytes 21798912 | tf_op jit(solution)/shard_map/dot_general | solution.py:160
  328.0 9.4 %collective-permute-done.70 = bf16[256,1024]{1,0:T(8,128)(2,1)S(1)} collective-permute-done((bf16[256,1024]{1,0:T(8,128)(2,1)S(1)}, bf16[256,1024]{1,0:T(8,128)(2,1)S(1)}, u32[]{:S(2)}, u32[]{:S(2)}) %collective-permute-start.70) | collective-permute-done | bytes 524320 | tf_op jit(solution)/shard_map/ppermute | solution.py:70
  367.3 15.1 %collective-permute-done.40 = bf16[256,2624]{0,1:T(8,128)(2,1)} collective-permute-done((bf16[256,2624]{0,1:T(8,128)(2,1)S(1)}, bf16[256,2624]{0,1:T(8,128)(2,1)}, u32[]{:S(2)}, u32[]{:S(2)}) %collective-permute-start.40) | collective-permute-done | bytes 1343520 | tf_op jit(solution)/shard_map/ppermute | solution.py:70
  383.9 6.3 %multiply_reduce_fusion = (f32[16,320]{1,0:T(8,128)S(1)}, f32[16,320,448]{2,1,0:T(8,128)S(1)}) fusion(f32[16,320,448]{2,1,0:T(8,128)} %get-tuple-element.221, f32[16,320]{1,0:T(8,128)S(1)} %copy-done.115, bf16[320,16,64]{0,2,1:T(8,128)(2,1)S(1)} %bitcast.300, bf16[448,16,64]{0,2,1:T(8,128)(2,1)S(1)} %bitcast.299), kind=kOutput, calls=%fused_computation.2 | convolution fusion | flops 300477440 | bytes 19963904 | tf_op jit(solution)/shard_map/while/body/eval_jaxpr/qhd,khd->hqk/dot_general | solution.py:311
  403.3 6.9 %collective-permute-done.46 = bf16[256,2624]{0,1:T(8,128)(2,1)S(1)} collective-permute-done((bf16[256,2624]{0,1:T(8,128)(2,1)}, bf16[256,2624]{0,1:T(8,128)(2,1)S(1)}, u32[]{:S(2)}, u32[]{:S(2)}) %collective-permute-start.46) | collective-permute-done | bytes 1343520 | tf_op jit(solution)/shard_map/ppermute | solution.py:70
  426.8 5.4 collective-permute-start.47
  446.3 6.3 %scatter-add.6 = f32[320,2048]{0,1:T(8,128)} dynamic-update-slice(f32[320,2048]{0,1:T(8,128)} %fusion.21, f32[64,2048]{0,1:T(8,128)S(1)} %fusion.76, s32[]{:T(128)} %constant.185.clone.1, s32[]{:T(128)} %constant.185.clone.1) | dynamic-update-slice | bytes 1048580 | tf_op jit(solution)/shard_map/scatter-add | solution.py:348
  475.5 7.7 %collective-permute-start.49 = (f32[16,2,32]{2,1,0:T(2,128)S(1)}, f32[16,2,32]{2,1,0:T(2,128)S(1)}, u32[]{:S(2)}, u32[]{:S(2)}) collective-permute-start(f32[16,2,32]{2,1,0:T(2,128)S(1)} %slice.660), channel_id=1, source_target_pairs={{0,4},{1,5},{2,6},{3,7},{4,0},{5,1},{6,2},{7,3},{8,12},{9,13},{10,... | collective-permute-start | bytes 12296 | tf_op jit(solution)/shard_map/ppermute | solution.py:70
  516.8 5.9 collective-permute-done.85
  523.5 10.6 %collective-permute-start.80 = (bf16[32,2624]{1,0:T(8,128)(2,1)S(1)}, bf16[32,2624]{1,0:T(8,128)(2,1)S(1)}, u32[]{:S(2)}, u32[]{:S(2)}) collective-permute-start(bf16[32,2624]{1,0:T(8,128)(2,1)S(1)} %get-tuple-element.166), channel_id=1, source_target_pairs={{0,1},{1,0},{2,3},{3,2},{4,5},{5,4},{6,7},{7,6},{8,9},{9,8},{10,11... | collective-permute-start | bytes 503816 | tf_op jit(solution)/shard_map/ppermute | solution.py:70
  538.9 6.4 %collective-permute-done.82 = bf16[32,2624]{1,0:T(8,128)(2,1)S(1)} collective-permute-done((bf16[32,2624]{1,0:T(8,128)(2,1)S(1)}, bf16[32,2624]{1,0:T(8,128)(2,1)S(1)}, u32[]{:S(2)}, u32[]{:S(2)}) %collective-permute-start.82) | collective-permute-done | bytes 167968 | tf_op jit(solution)/shard_map/ppermute | solution.py:70
  557.1 12.7 %collective-permute-done.63 = bf16[256,1536]{1,0:T(8,128)(2,1)S(1)} collective-permute-done((bf16[256,1536]{1,0:T(8,128)(2,1)S(1)}, bf16[256,1536]{1,0:T(8,128)(2,1)S(1)}, u32[]{:S(2)}, u32[]{:S(2)}) %collective-permute-start.63) | collective-permute-done | bytes 786464 | tf_op jit(solution)/shard_map/ppermute | solution.py:70
  573.2 7.2 %collective-permute-done.64 = bf16[1,4,32,1536]{3,2,1,0:T(8,128)(2,1)S(1)} collective-permute-done((bf16[1,4,32,1536]{3,2,1,0:T(8,128)(2,1)S(1)}, bf16[1,4,32,1536]{3,2,1,0:T(8,128)(2,1)S(1)}, u32[]{:S(2)}, u32[]{:S(2)}) %collective-permute-start.64) | collective-permute-done | bytes 393248 | tf_op jit(solution)/shard_map/ppermute | solution.py:70
  591.3 6.7 %collective-permute-done.66 = bf16[32,1536]{1,0:T(8,128)(2,1)S(1)} collective-permute-done((bf16[32,1536]{1,0:T(8,128)(2,1)S(1)}, bf16[32,1536]{1,0:T(8,128)(2,1)S(1)}, u32[]{:S(2)}, u32[]{:S(2)}) %collective-permute-start.66) | collective-permute-done | bytes 98336 | tf_op jit(solution)/shard_map/ppermute | solution.py:70
  (639 shorter events, 408.0 us)
Async XLA Ops:
  62.1 23.0 %collective-permute-start.21 = (bf16[32,2624]{1,0:T(8,128)(2,1)S(1)}, bf16[32,2624]{1,0:T(8,128)(2,1)S(1)}, u32[]{:S(2)}, u32[]{:S(2)}) collective-permute-start(bf16[32,2624]{1,0:T(8,128)(2,1)S(1)} %get-tuple-element.200), channel_id=1, source_target_pairs={{0,2},{1,3},{2,0},{3,1},{4,6},{5,7},{6,4},{7,5},{8,10},{9,11},{10,... | collective-permute-start | bytes 503816 | tf_op jit(solution)/shard_map/ppermute | solution.py:70
  62.8 22.4 %collective-permute-start.20 = (bf16[32,2624]{1,0:T(8,128)(2,1)S(1)}, bf16[32,2624]{1,0:T(8,128)(2,1)S(1)}, u32[]{:S(2)}, u32[]{:S(2)}) collective-permute-start(bf16[32,2624]{1,0:T(8,128)(2,1)S(1)} %get-tuple-element.200), channel_id=1, source_target_pairs={{0,1},{1,0},{2,3},{3,2},{4,5},{5,4},{6,7},{7,6},{8,9},{9,8},{10,11... | collective-permute-start | bytes 503816 | tf_op jit(solution)/shard_map/ppermute | solution.py:70
  85.2 46.9 %collective-permute-start.10 = (bf16[512,1664]{0,1:T(8,128)(2,1)}, bf16[512,1664]{0,1:T(8,128)(2,1)}, u32[]{:S(2)}, u32[]{:S(2)}) collective-permute-start(bf16[512,1664]{0,1:T(8,128)(2,1)} %copy.112), channel_id=1, source_target_pairs={{0,4},{1,5},{2,6},{3,7},{4,0},{5,1},{6,2},{7,3},{8,12},{9,13},{10,... | collective-permute-start | bytes 5111816 | tf_op jit(solution)/shard_map/ppermute | solution.py:70
  97.1 40.4 %collective-permute-start.11 = (bf16[512,1536]{1,0:T(8,128)(2,1)}, bf16[512,1536]{1,0:T(8,128)(2,1)}, u32[]{:S(2)}, u32[]{:S(2)}) collective-permute-start(bf16[512,1536]{1,0:T(8,128)(2,1)} %bitcast.284), channel_id=1, source_target_pairs={{0,4},{1,5},{2,6},{3,7},{4,0},{5,1},{6,2},{7,3},{8,12},{9,13},{10,... | collective-permute-start | bytes 4718600 | tf_op jit(solution)/shard_map/ppermute | solution.py:70
  101.3 25.0 %collective-permute-start.18 = (bf16[1,2,128,1024]{3,2,1,0:T(8,128)(2,1)}, bf16[1,2,128,1024]{3,2,1,0:T(8,128)(2,1)}, u32[]{:S(2)}, u32[]{:S(2)}) collective-permute-start(bf16[1,2,128,1024]{3,2,1,0:T(8,128)(2,1)} %pad_maximum_fusion.19), channel_id=1, source_target_pairs={{0,16},{1,17},{2,18},{3,19},{4,20},{5,21},{6,22},{7,23},{8,24},{9,... | collective-permute-start | bytes 1572872 | tf_op jit(solution)/shard_map/ppermute | solution.py:70
  116.2 49.4 %collective-permute-start.24 = (bf16[1,2,128,2624]{2,3,1,0:T(8,128)(2,1)}, bf16[1,2,128,2624]{2,3,1,0:T(8,128)(2,1)}, u32[]{:S(2)}, u32[]{:S(2)}) collective-permute-start(bf16[1,2,128,2624]{2,3,1,0:T(8,128)(2,1)} %copy.121), channel_id=1, source_target_pairs={{0,16},{1,17},{2,18},{3,19},{4,20},{5,21},{6,22},{7,23},{8,24},{9,... | collective-permute-start | bytes 4030472 | tf_op jit(solution)/shard_map/ppermute | solution.py:70
  124.8 44.7 %collective-permute-start.29 = (bf16[2,1,128,2624]{2,3,1,0:T(8,128)(2,1)}, bf16[2,1,128,2624]{2,3,1,0:T(8,128)(2,1)}, u32[]{:S(2)}, u32[]{:S(2)}) collective-permute-start(bf16[2,1,128,2624]{2,3,1,0:T(8,128)(2,1)} %copy.125), channel_id=1, source_target_pairs={{0,8},{1,9},{2,10},{3,11},{4,12},{5,13},{6,14},{7,15},{8,0},{9,1},... | collective-permute-start | bytes 4030472 | tf_op jit(solution)/shard_map/ppermute | solution.py:70
  128.5 33.5 %collective-permute-start.19 = (bf16[512,1024]{1,0:T(8,128)(2,1)}, bf16[512,1024]{1,0:T(8,128)(2,1)}, u32[]{:S(2)}, u32[]{:S(2)}) collective-permute-start(bf16[512,1024]{1,0:T(8,128)(2,1)} %bitcast.17), channel_id=1, source_target_pairs={{0,4},{1,5},{2,6},{3,7},{4,0},{5,1},{6,2},{7,3},{8,12},{9,13},{10,... | collective-permute-start | bytes 3145736 | tf_op jit(solution)/shard_map/ppermute | solution.py:70
  221.2 30.9 %collective-permute-start.36 = (bf16[2,1,128,2624]{2,3,1,0:T(8,128)(2,1)}, bf16[2,1,128,2624]{2,3,1,0:T(8,128)(2,1)}, u32[]{:S(2)}, u32[]{:S(2)}) collective-permute-start(bf16[2,1,128,2624]{2,3,1,0:T(8,128)(2,1)} %copy.131), channel_id=1, source_target_pairs={{0,8},{1,9},{2,10},{3,11},{4,12},{5,13},{6,14},{7,15},{8,0},{9,1},... | collective-permute-start | bytes 4030472 | tf_op jit(solution)/shard_map/ppermute | solution.py:70
  234.8 33.9 %collective-permute-start.31 = (bf16[512,2624]{0,1:T(8,128)(2,1)}, bf16[512,2624]{0,1:T(8,128)(2,1)}, u32[]{:S(2)}, u32[]{:S(2)}) collective-permute-start(bf16[512,2624]{0,1:T(8,128)(2,1)} %copy.128), channel_id=1, source_target_pairs={{0,4},{1,5},{2,6},{3,7},{4,0},{5,1},{6,2},{7,3},{8,12},{9,13},{10,... | collective-permute-start | bytes 8060936 | tf_op jit(solution)/shard_map/ppermute | solution.py:70
  242.2 29.4 %collective-permute-start.30 = (bf16[512,2624]{0,1:T(8,128)(2,1)}, bf16[512,2624]{0,1:T(8,128)(2,1)}, u32[]{:S(2)}, u32[]{:S(2)}) collective-permute-start(bf16[512,2624]{0,1:T(8,128)(2,1)} %copy.127), channel_id=1, source_target_pairs={{0,4},{1,5},{2,6},{3,7},{4,0},{5,1},{6,2},{7,3},{8,12},{9,13},{10,... | collective-permute-start | bytes 8060936 | tf_op jit(solution)/shard_map/ppermute | solution.py:70
  315.9 37.5 %collective-permute-start.38 = (bf16[256,2624]{0,1:T(8,128)(2,1)S(1)}, bf16[256,2624]{0,1:T(8,128)(2,1)S(1)}, u32[]{:S(2)}, u32[]{:S(2)}) collective-permute-start(bf16[256,2624]{0,1:T(8,128)(2,1)S(1)} %copy-done.66), channel_id=1, source_target_pairs={{0,4},{1,5},{2,6},{3,7},{4,0},{5,1},{6,2},{7,3},{8,12},{9,13},{10,... | collective-permute-start | bytes 4030472 | tf_op jit(solution)/shard_map/ppermute | solution.py:70
  316.4 32.5 %collective-permute-start.39 = (bf16[256,2624]{0,1:T(8,128)(2,1)S(1)}, bf16[256,2624]{0,1:T(8,128)(2,1)S(1)}, u32[]{:S(2)}, u32[]{:S(2)}) collective-permute-start(bf16[256,2624]{0,1:T(8,128)(2,1)S(1)} %copy-done.68), channel_id=1, source_target_pairs={{0,4},{1,5},{2,6},{3,7},{4,0},{5,1},{6,2},{7,3},{8,12},{9,13},{10,... | collective-permute-start | bytes 4030472 | tf_op jit(solution)/shard_map/ppermute | solution.py:70
  317.5 28.2 %collective-permute-start.41 = (bf16[256,2624]{0,1:T(8,128)(2,1)S(1)}, bf16[256,2624]{0,1:T(8,128)(2,1)S(1)}, u32[]{:S(2)}, u32[]{:S(2)}) collective-permute-start(bf16[256,2624]{0,1:T(8,128)(2,1)S(1)} %convolution_convert_fusion.3), channel_id=1, source_target_pairs={{0,4},{1,5},{2,6},{3,7},{4,0},{5,1},{6,2},{7,3},{8,12},{9,13},{10,... | collective-permute-start | bytes 4030472 | tf_op jit(solution)/shard_map/ppermute | solution.py:70
  349.9 32.5 %collective-permute-start.40 = (bf16[256,2624]{0,1:T(8,128)(2,1)S(1)}, bf16[256,2624]{0,1:T(8,128)(2,1)}, u32[]{:S(2)}, u32[]{:S(2)}) collective-permute-start(bf16[256,2624]{0,1:T(8,128)(2,1)S(1)} %add_convert_fusion.3), channel_id=1, source_target_pairs={{0,16},{1,17},{2,18},{3,19},{4,20},{5,21},{6,22},{7,23},{8,24},{9,... | collective-permute-start | bytes 4030472 | tf_op jit(solution)/shard_map/ppermute | solution.py:70
  362.0 48.2 %collective-permute-start.46 = (bf16[256,2624]{0,1:T(8,128)(2,1)}, bf16[256,2624]{0,1:T(8,128)(2,1)S(1)}, u32[]{:S(2)}, u32[]{:S(2)}) collective-permute-start(bf16[256,2624]{0,1:T(8,128)(2,1)} %add_convert_fusion.1), channel_id=1, source_target_pairs={{0,16},{1,17},{2,18},{3,19},{4,20},{5,21},{6,22},{7,23},{8,24},{9,... | collective-permute-start | bytes 4030472 | tf_op jit(solution)/shard_map/ppermute | solution.py:70
  365.2 45.0 %collective-permute-start.43 = (bf16[256,2624]{0,1:T(8,128)(2,1)}, bf16[256,2624]{0,1:T(8,128)(2,1)}, u32[]{:S(2)}, u32[]{:S(2)}) collective-permute-start(bf16[256,2624]{0,1:T(8,128)(2,1)} %add_convert_fusion.2), channel_id=1, source_target_pairs={{0,8},{1,9},{2,10},{3,11},{4,12},{5,13},{6,14},{7,15},{8,0},{9,1},... | collective-permute-start | bytes 4030472 | tf_op jit(solution)/shard_map/ppermute | solution.py:70
  421.2 79.8 %collective-permute-start.83 = (bf16[1,4,32,2624]{3,2,1,0:T(8,128)(2,1)}, bf16[1,4,32,2624]{3,2,1,0:T(8,128)(2,1)}, u32[]{:S(2)}, u32[]{:S(2)}) collective-permute-start(bf16[1,4,32,2624]{3,2,1,0:T(8,128)(2,1)} %bitcast.303), channel_id=1, source_target_pairs={{0,8},{1,9},{2,10},{3,11},{4,12},{5,13},{6,14},{7,15},{8,0},{9,1},... | collective-permute-start | bytes 2015240 | tf_op jit(solution)/shard_map/ppermute | solution.py:70
  425.5 27.0 %collective-permute-start.48 = (bf16[64,2048]{0,1:T(8,128)(2,1)}, bf16[64,2048]{0,1:T(8,128)(2,1)}, u32[]{:S(2)}, u32[]{:S(2)}) collective-permute-start(bf16[64,2048]{0,1:T(8,128)(2,1)} %get-tuple-element.144), channel_id=1, source_target_pairs={{1,0},{2,1},{3,2},{4,3},{5,4},{6,5},{7,6},{8,7},{9,8},{10,9},{11,1... | collective-permute-start | bytes 786440 | tf_op jit(solution)/shard_map/ppermute | solution.py:30
  435.9 68.1 %collective-permute-start.75 = (bf16[1,4,32,2624]{3,2,1,0:T(8,128)(2,1)}, bf16[1,4,32,2624]{3,2,1,0:T(8,128)(2,1)}, u32[]{:S(2)}, u32[]{:S(2)}) collective-permute-start(bf16[1,4,32,2624]{3,2,1,0:T(8,128)(2,1)} %bitcast.304), channel_id=1, source_target_pairs={{0,16},{1,17},{2,18},{3,19},{4,20},{5,21},{6,22},{7,23},{8,24},{9,... | collective-permute-start | bytes 2015240 | tf_op jit(solution)/shard_map/ppermute | solution.py:70
  439.8 67.9 %collective-permute-start.79 = (bf16[1,4,32,2624]{3,2,1,0:T(8,128)(2,1)}, bf16[1,4,32,2624]{3,2,1,0:T(8,128)(2,1)}, u32[]{:S(2)}, u32[]{:S(2)}) collective-permute-start(bf16[1,4,32,2624]{3,2,1,0:T(8,128)(2,1)} %bitcast.302), channel_id=1, source_target_pairs={{0,8},{1,9},{2,10},{3,11},{4,12},{5,13},{6,14},{7,15},{8,0},{9,1},... | collective-permute-start | bytes 2015240 | tf_op jit(solution)/shard_map/ppermute | solution.py:70
  486.9 63.0 %collective-permute-start.62 = (bf16[256,1536]{1,0:T(8,128)(2,1)S(1)}, bf16[256,1536]{1,0:T(8,128)(2,1)S(1)}, u32[]{:S(2)}, u32[]{:S(2)}) collective-permute-start(bf16[256,1536]{1,0:T(8,128)(2,1)S(1)} %convolution_convert_fusion.6), channel_id=1, source_target_pairs={{0,4},{1,5},{2,6},{3,7},{4,0},{5,1},{6,2},{7,3},{8,12},{9,13},{10,... | collective-permute-start | bytes 2359304 | tf_op jit(solution)/shard_map/ppermute | solution.py:70
  500.5 56.6 %collective-permute-start.61 = (bf16[256,1536]{1,0:T(8,128)(2,1)S(1)}, bf16[256,1536]{1,0:T(8,128)(2,1)S(1)}, u32[]{:S(2)}, u32[]{:S(2)}) collective-permute-start(bf16[256,1536]{1,0:T(8,128)(2,1)S(1)} %convolution_convert_fusion.7), channel_id=1, source_target_pairs={{0,4},{1,5},{2,6},{3,7},{4,0},{5,1},{6,2},{7,3},{8,12},{9,13},{10,... | collective-permute-start | bytes 2359304 | tf_op jit(solution)/shard_map/ppermute | solution.py:70
  545.2 26.1 %collective-permute-start.54 = (bf16[256,1536]{1,0:T(8,128)(2,1)S(1)}, bf16[256,1536]{1,0:T(8,128)(2,1)S(1)}, u32[]{:S(2)}, u32[]{:S(2)}) collective-permute-start(bf16[256,1536]{1,0:T(8,128)(2,1)S(1)} %convolution_convert_fusion.9), channel_id=1, source_target_pairs={{0,4},{1,5},{2,6},{3,7},{4,0},{5,1},{6,2},{7,3},{8,12},{9,13},{10,... | collective-permute-start | bytes 2359304 | tf_op jit(solution)/shard_map/ppermute | solution.py:70
  (195 other events, 2097.1 us)
